TPU v7x, 256 devices: a whole 4x4x8 slice. The times are simulated.
256 devices in a mesh: section: 2 (over core), kv: 32 (over z, x), head: 4 (over y).
Axes of the slice: x: 4, y: 4, z: 8, core: 2. Of those that a mesh axis runs over, the one named last changes fastest.
Arguments:
- queries: bfloat16 [16, 128, 576], P('section', 'head'), may hold values from -180 to 180
- cache: bfloat16 [4096, 128, 576], P(('section', 'kv')), may hold values from -8 to 8
- slot_request: int32 [4096], P(('section', 'kv')), may hold values from -1 to 15, as said below
- slot_page: int32 [4096], P(('section', 'kv')), may hold values from 0 to 255
- lengths: int32 [16], P('section'), may hold values from 4096 to 32768, as said below
- w_uv: bfloat16 [128, 512, 128], P('head'), may hold values from -3 to 3
- w_out: bfloat16 [16384, 7168], P('head', ('section', 'kv')), may hold values from -0.046875 to 0.046875
- hidden: bfloat16 [16, 7168], P(None, ('section', 'kv')), may hold values from -6 to 6
Outputs:
- mixed: bfloat16 [16, 7168], P(None, ('section', 'kv'))
Inputs may be any that keep to these rules, and one draw needn't show every extreme that they name: `slot_request`: requests b with b // 8 = i have their pages only in slots of index i of section; each such request owns exactly one slot for each page number below ceil(lengths[b] / 128) and no other; the remaining slots are -1. `lengths`: in every index of section one request holds exactly 32768 tokens.
All inputs are finite; a program needn't handle non-finite values.
Results may differ from a plain program's by a relative error of at most 0.015.
Values may be sent and summed in bfloat16 or wider, within the bound.
No kernel may reach another device: no remote copies, remote signals or barrier semaphores. Data moves between devices by JAX's collectives and lax.ppermute only.
A program may use at most 128 MiB of HBM per device.

v0:
```python
import jax
import jax.numpy as jnp
from jax import lax
from jax.sharding import PartitionSpec as P

ROPE = 64
NOPE = 128


def combined_all(array, axis, combine):
    everything = jax.tree.map(lambda part: lax.all_gather(part, axis), array)
    first = jax.tree.map(lambda part: part[0], everything)

    def lap(k, so_far):
        return combine(so_far, jax.tree.map(lambda part: part[k], everything))

    return lax.fori_loop(1, lax.axis_size(axis), lap, first)


def combine(earlier, later):
    high_a, denom_a, summed_a = earlier
    high_b, denom_b, summed_b = later
    highest = jnp.maximum(high_a, high_b)
    factor_a = jnp.exp(high_a - highest)
    factor_b = jnp.exp(high_b - highest)
    return (
        highest,
        denom_a * factor_a + denom_b * factor_b,
        summed_a * factor_a[..., None] + summed_b * factor_b[..., None],
    )


def value_project(latent, weights):
    return jnp.einsum(
        "rhl,hlv->rhv", latent, weights.astype(jnp.float32), precision=lax.Precision.HIGHEST
    )


def body(queries, cache, slot_request, slot_page, lengths, w_uv, w_out, hidden):
    requests = queries.shape[0]
    heads = queries.shape[1]
    latent_width = w_uv.shape[1]
    value_width = w_uv.shape[2]
    slot_count = cache.shape[0]
    page_size = cache.shape[1]
    scale = (NOPE + ROPE) ** (-0.5)
    local = slot_request - lax.axis_index("section") * requests
    owned = (local >= 0) & (local < requests)
    index = jnp.clip(local, 0, requests - 1)
    gathered = queries[index]
    scores = jnp.einsum("shw,stw->sht", gathered, cache, preferred_element_type=jnp.float32) * scale
    position = slot_page[:, None] * page_size + jnp.arange(page_size)[None, :]
    valid = owned[:, None] & (position < lengths[index][:, None])
    scores = jnp.where(valid[:, None, :], scores, -1e30)
    onehot = (index[None, :] == jnp.arange(requests)[:, None]) & owned[None, :]
    slot_high = jnp.max(scores, axis=2)
    highest = jnp.max(jnp.where(onehot[:, :, None], slot_high[None, :, :], -1e30), axis=1)
    weights = jnp.exp(scores - highest[index][:, :, None])
    probs = weights.astype(jnp.bfloat16)
    slot_denom = jnp.sum(weights, axis=2)
    slot_summed = jnp.einsum(
        "sht,stl->shl", probs, cache[:, :, :latent_width], preferred_element_type=jnp.float32
    )
    selector = onehot.astype(jnp.float32)
    denom = jnp.dot(selector, slot_denom, precision=lax.Precision.HIGHEST)
    summed = jnp.dot(
        selector,
        slot_summed.reshape(slot_count, heads * latent_width),
        precision=lax.Precision.HIGHEST,
    ).reshape(requests, heads, latent_width)
    carried = summed
    highest, denom, carried = combined_all((highest, denom, carried), "kv", combine)
    finished = carried / denom[..., None]
    heads_out = value_project(finished, w_uv).astype(jnp.bfloat16)
    heads_out = heads_out.reshape(requests, heads * value_width)
    projected = jnp.dot(
        lax.all_gather(heads_out, "section", axis=0, tiled=True),
        w_out,
        preferred_element_type=jnp.float32,
    )
    projected = lax.psum(projected, "head")
    return (hidden.astype(jnp.float32) + projected).astype(jnp.bfloat16)


def solution(mesh):
    placed = (
        P("section", "head", None),
        P(("section", "kv"), None, None),
        P(("section", "kv")),
        P(("section", "kv")),
        P("section"),
        P("head", None, None),
        P("head", ("section", "kv")),
        P(None, ("section", "kv")),
    )
    return jax.shard_map(
        body, mesh=mesh, in_specs=placed, out_specs=P(None, ("section", "kv")), check_vma=False
    )
```

profile of v0, /device:TPU:1, one launch (start us, length us, event | category | flops | bytes accessed | tf_op | source)
XLA Modules:
  0.0 254.8 jit_solution(833172999684943688)
XLA Ops:
  6.5 1.6 fusion.26
  8.8 5.6 %compare_select_fusion.1 = (s32[64]{0:T(128)S(1)}, s32[64]{0:T(128)S(1)}, s32[64]{0:T(128)S(1)}) fusion(s32[]{:T(128)} %bitcast.3, s32[]{:T(128)} %bitcast.4, s32[]{:T(128)} %bitcast.5, s32[]{:T(128)} %bitcast.6, s32[]{:T(128)} %bitcast.7, s32[]{:T(128)} %bitcast.8, s32[]{:T(128)} %bitcast.9, s32[]{:T(128)} %bitcast.10, s32[64]{0:T(128)} %param.12, ...), kind=kLoop, calls=%fused_computation.39 | loop fusion | flops 1280 | bytes 1316 | tf_op jit(solution)/shard_map/gather | solution.py:53
  15.7 2.1 gather_fusion
  17.8 6.9 %fusion.27 = (f32[64,32]{1,0:T(8,128)}, f32[64,32,128]{2,1,0:T(8,128)}) fusion(bf16[64,32,576]{2,1,0:T(8,128)(2,1)S(1)} %gather_fusion, bf16[64,128,576]{1,2,0:T(8,128)(2,1)} %param.11, pred[64,128]{1,0:T(8,128)(4,1)S(1)} %fusion.16), kind=kOutput, calls=%fused_computation.52 | convolution fusion | flops 302774272 | bytes 12861440 | tf_op jit(solution)/shard_map/shw,stw->sht/dot_general | solution.py:51
  27.1 6.7 %fusion.4 = f32[64,32,512]{2,1,0:T(8,128)S(1)} fusion(bf16[64,128,576]{1,2,0:T(8,128)(2,1)} %param.11, f32[64,32,128]{2,1,0:T(8,128)} %get-tuple-element.241, f32[64,32]{1,0:T(8,128)S(1)} %gather_fusion.1), kind=kOutput, calls=%fused_computation.12 | convolution fusion | flops 268959744 | bytes 13639680 | tf_op jit(solution)/shard_map/sht,stl->shl/dot_general | solution.py:61
  33.8 4.6 %fusion.6 = f32[8,32,512]{2,0,1:T(8,128)} fusion(s32[64]{0:T(128)S(1)} %get-tuple-element.231, pred[64]{0:T(512)(128)(4,1)S(1)} %compare_and_fusion, f32[8,8,32,512]{3,2,1,0:T(8,128)S(1)} %bitcast.58), kind=kOutput, calls=%fused_computation.14 | convolution fusion | flops 100664320 | bytes 4718912 | tf_op jit(solution)/shard_map/dot_general | solution.py:66
  39.3 40.3 %all-gather.1 = f32[256,32]{1,0:T(8,128)S(1)} all-gather(f32[8,32]{1,0:T(8,128)S(1)} %fusion.23), channel_id=3, replica_groups=mesh['section'=2,'kv'=32,'head'=4] {'kv'}, dimensions={0}, use_global_device_ids=true | all-gather | bytes 33792 | tf_op jit(solution)/shard_map/all_gather | solution.py:11
  79.6 35.2 %all-gather = f32[256,32]{1,0:T(8,128)S(1)} all-gather(f32[8,32]{1,0:T(8,128)S(1)} %select_reduce_fusion), channel_id=2, replica_groups=mesh['section'=2,'kv'=32,'head'=4] {'kv'}, dimensions={0}, use_global_device_ids=true | all-gather | bytes 33792 | tf_op jit(solution)/shard_map/all_gather | solution.py:11
  114.8 68.2 %all-gather.5.cloned.1.call-done = f32[256,32,512]{2,0,1:T(8,128)} async-done(((f32[8,32,512]{2,0,1:T(8,128)}), f32[256,32,512]{2,0,1:T(8,128)}) %all-gather.5.cloned.1.call-update) | async-done | bytes 16777232 | tf_op jit(solution)/shard_map/all_gather | solution.py:11
  184.4 47.6 %while.19 = (s32[]{:T(128)}, f32[8,32]{1,0:T(8,128)S(1)}, f32[8,32]{1,0:T(8,128)S(1)}, f32[8,32,512]{2,1,0:T(8,128)S(1)}, f32[32,8,32]{2,1,0:T(8,128)S(1)}, /*in...) while((s32[]{:T(128)}, f32[8,32]{1,0:T(8,128)S(1)}, ...), condition=%wide.region_4.5_spmd, body=%wide.region_3.4_spmd.sunk | while | flops 394757 | bytes 2631823 | solution.py:17
  184.4 1.1 constant_dynamic-slice_fusion.2
  186.0 1.1 constant_dynamic-slice_fusion.2
  187.5 1.1 constant_dynamic-slice_fusion.2
  189.1 1.1 constant_dynamic-slice_fusion.2
  190.6 1.1 constant_dynamic-slice_fusion.2
  192.1 1.1 constant_dynamic-slice_fusion.2
  193.7 1.1 constant_dynamic-slice_fusion.2
  195.2 1.1 constant_dynamic-slice_fusion.2
  196.7 1.1 constant_dynamic-slice_fusion.2
  198.3 1.1 constant_dynamic-slice_fusion.2
  201.3 1.1 constant_dynamic-slice_fusion.2
  204.4 1.1 constant_dynamic-slice_fusion.2
  205.9 1.1 constant_dynamic-slice_fusion.2
  207.5 1.1 constant_dynamic-slice_fusion.2
  209.0 1.1 constant_dynamic-slice_fusion.2
  210.6 1.1 constant_dynamic-slice_fusion.2
  212.1 1.1 constant_dynamic-slice_fusion.2
  213.6 1.1 constant_dynamic-slice_fusion.2
  215.2 1.1 constant_dynamic-slice_fusion.2
  232.1 3.8 %fusion.10 = bf16[8,4096]{1,0:T(8,128)(2,1)S(1)} fusion(bf16[32,512,128]{2,1,0:T(8,128)(2,1)} %param.15, f32[8,32,512]{2,1,0:T(8,128)S(1)} %broadcast_divide_fusion), kind=kOutput, calls=%fused_computation.20 | convolution fusion | flops 201359360 | bytes 4784128 | tf_op jit(solution)/shard_map/rhl,hlv->rhv/dot_general | solution.py:34
  235.9 2.5 all_gather.23
  238.8 8.6 %psum.7 = f32[16,112]{1,0:T(8,128)S(1)} all-reduce(f32[16,112]{1,0:T(8,128)S(1)} %fusion.28), channel_id=1, replica_groups=mesh['section'=2,'kv'=32,'head'=4] {'head'}, use_global_device_ids=true, to_apply=%region_5.6 | all-reduce | flops 1792 | bytes 14336 | tf_op jit(solution)/shard_map/psum | solution.py:81
  (99 shorter events, 33.5 us)
Async XLA Ops:
  6.5 232.0 %copy-start = (bf16[4096,112]{0,1:T(8,128)(2,1)S(1)}, bf16[4096,112]{0,1:T(8,128)(2,1)}, u32[]{:S(2)}) copy-start(bf16[4096,112]{0,1:T(8,128)(2,1)} %param.16) | copy-start | bytes 2752516
  6.5 176.5 %all-gather.5.cloned.1.call-start = ((), (), s32[]{:S(2)}) async-start(), calls=%async_computation | async-start | bytes 17301504 | tf_op jit(solution)/shard_map/all_gather | solution.py:11
  33.8 4.7 %copy-start.1 = (f32[64,32,128]{2,1,0:T(8,128)S(1)}, f32[64,32,128]{2,1,0:T(8,128)}, u32[]{:S(2)}) copy-start(f32[64,32,128]{2,1,0:T(8,128)} %get-tuple-element.241) | copy-start | bytes 3145732
  232.0 15.4 %copy-start.2 = (bf16[16,112]{1,0:T(8,128)(2,1)S(1)}, bf16[16,112]{1,0:T(8,128)(2,1)}, u32[]{:S(2)}) copy-start(bf16[16,112]{1,0:T(8,128)(2,1)} %param.17) | copy-start | bytes 10756
Sparse Core Ops, SparseCore 0:
  38.6 144.3 all-gather.4
where the time goes:
time: 257 us; the launch traced here: 255 us
  blocking collectives  86.7 us (34%)
  waiting for transfers between devices  68.2 us (27%)
  local copies, waits for them, and re-layouts  40.2 us (16%)
  other arithmetic  22.7 us (9%)
  matrix products  22.6 us (9%)
  between operations  13.5 us (5%)
    all_gather x2, blocking collectives, combined_all(): everything = jax.tree.map(lambda part: lax.all_gather(part, axis), array)  75.6 us
    all_gather x1, waiting for transfers between devices, combined_all(): everything = jax.tree.map(lambda part: lax.all_gather(part, axis), array)  68.2 us
    dynamic_slice x31, local copies, waits for them, and re-layouts, lap(): return combine(so_far, jax.tree.map(lambda part: part[k], everything))  33.6 us
    add x31, other arithmetic, combine(): summed_a * factor_a[..., None] + summed_b * factor_b[..., None]  12.5 us
    psum x1, blocking collectives, body(): projected = lax.psum(projected, 'head')  8.55 us
    dot_general x1, matrix products, body(): jnp.einsum('shw,stw->sht', gathered, cache, preferred_element_type=jnp.fl...  6.94 us
    dot_general x1, matrix products, body(): jnp.einsum('sht,stl->shl', probs, cache[:, :, :latent_width], preferred_e...  6.74 us
    gather x1, other arithmetic, body(): valid = owned[:, None] & (position < lengths[index][:, None])  5.62 us
  transfers between devices with their start and end apart: 1, of which 1 were waited for; matrix products, arithmetic and copies ran while one was open for 0% of the time, Pallas kernels for 0%

commit v1 on v0

v1 whole, which is shorter than its diff:
```python
import functools

import jax
import jax.numpy as jnp
from jax import lax
from jax.experimental import pallas as pl
from jax.experimental.pallas import tpu as pltpu
from jax.sharding import PartitionSpec as P

ROPE = 64
NOPE = 128
LOWEST = -1e30
UNROLL = 4
AUX = 128
MIB = 1024 * 1024


def parts_of(value):
    high = value.astype(jnp.bfloat16).astype(jnp.float32)
    rest = value - high
    middle = rest.astype(jnp.bfloat16).astype(jnp.float32)
    return high, middle, rest - middle


def attend_kernel(
    owner_ref, page_ref, length_ref, query_ref, cache_ref, out_ref,
    pages, scores, high, denom, summed, packed, slots, owners, counts, sems,
):
    slot_count = cache_ref.shape[0]
    page_size = cache_ref.shape[2]
    requests, heads, _ = query_ref.shape
    latent = summed.shape[2]
    scale = (NOPE + ROPE) ** (-0.5)

    def copy(slot):
        return pltpu.make_async_copy(cache_ref.at[slot], pages.at[slot], sems.at[slot])

    def find(slot, found):
        owner = owner_ref[slot]

        @pl.when(owner >= 0)
        def _():
            copy(slot).start()
            mine = lax.rem(owner, requests)
            slots[found] = slot
            owners[found] = mine
            counts[found] = length_ref[mine] - page_ref[slot] * page_size

        return jnp.where(owner >= 0, found + 1, found)

    live = lax.fori_loop(0, slot_count, find, jnp.int32(0))
    blocks = lax.div(live + (UNROLL - 1), jnp.int32(UNROLL))

    high[...] = jnp.full(high.shape, LOWEST, jnp.float32)
    denom[...] = jnp.zeros(denom.shape, jnp.float32)
    summed[...] = jnp.zeros(summed.shape, jnp.float32)
    column = lax.broadcasted_iota(jnp.int32, (heads, page_size), 1)

    def score(block, carry):
        first = block * UNROLL
        for k in range(UNROLL):
            @pl.when(first + k < live)
            def _(k=k):
                copy(slots[first + k]).wait()
        for k in range(UNROLL):
            at = first + k
            entry = jnp.minimum(at, live - 1)
            mine = owners[entry]
            count = jnp.where(at < live, counts[entry], 0)
            found = jnp.dot(
                query_ref[mine], pages[slots[entry]], preferred_element_type=jnp.float32
            ) * scale
            found = jnp.where(column < count, found, LOWEST)
            scores[at] = found
            high[mine] = jnp.maximum(high[mine], found)
        return carry

    lax.fori_loop(0, blocks, score, 0)

    for mine in range(requests):
        top = jnp.max(high[mine], axis=1, keepdims=True)
        high[mine] = jnp.broadcast_to(top, (heads, page_size))

    def gather(block, carry):
        first = block * UNROLL
        for k in range(UNROLL):
            at = first + k
            entry = jnp.minimum(at, live - 1)
            mine = owners[entry]
            weights = jnp.exp(scores[at] - high[mine])
            weights = jnp.where(at < live, weights, 0.0)
            denom[mine] += weights
            summed[mine] += lax.dot_general(
                weights.astype(jnp.bfloat16),
                pages[slots[entry], :latent, :],
                (((1,), (1,)), ((), ())),
                preferred_element_type=jnp.float32,
            )
        return carry

    lax.fori_loop(0, blocks, gather, 0)

    lane = lax.broadcasted_iota(jnp.int32, (heads, AUX), 1)
    for mine in range(requests):
        packed[:, mine, :latent] = summed[mine]
        total = jnp.broadcast_to(jnp.sum(denom[mine], axis=1, keepdims=True), (heads, AUX))
        aux = jnp.zeros((heads, AUX), jnp.float32)
        for k, part in enumerate(parts_of(high[mine]) + parts_of(total)):
            aux = jnp.where(lane == k, part, aux)
        packed[:, mine, latent:] = aux
    out_ref[...] = packed[...].reshape(out_ref.shape).astype(jnp.bfloat16)


def attend(queries, cache, slot_request, slot_page, lengths, latent):
    requests, heads, width = queries.shape
    slot_count, page_size, _ = cache.shape
    padded = slot_count + UNROLL
    smem = pl.BlockSpec(memory_space=pltpu.SMEM)
    vmem = pl.BlockSpec(memory_space=pltpu.VMEM)
    return pl.pallas_call(
        attend_kernel,
        out_shape=jax.ShapeDtypeStruct((heads * requests, latent + AUX), jnp.bfloat16),
        in_specs=[smem, smem, smem, vmem, pl.BlockSpec(memory_space=pl.ANY)],
        out_specs=vmem,
        scratch_shapes=[
            pltpu.VMEM((slot_count, width, page_size), jnp.bfloat16),
            pltpu.VMEM((padded, heads, page_size), jnp.float32),
            pltpu.VMEM((requests, heads, page_size), jnp.float32),
            pltpu.VMEM((requests, heads, page_size), jnp.float32),
            pltpu.VMEM((requests, heads, latent), jnp.float32),
            pltpu.VMEM((heads, requests, latent + AUX), jnp.float32),
            pltpu.SMEM((padded,), jnp.int32),
            pltpu.SMEM((padded,), jnp.int32),
            pltpu.SMEM((padded,), jnp.int32),
            pltpu.SemaphoreType.DMA((slot_count,)),
        ],
        compiler_params=pltpu.CompilerParams(vmem_limit_bytes=40 * MIB),
        name="attend",
    )(slot_request, slot_page, lengths, queries, jnp.swapaxes(cache, 1, 2))


def value_kernel(copies, part_ref, weight_ref, out_ref, weight, sem):
    latent = weight.shape[0]
    sources = weight_ref.shape[0]
    requests = part_ref.shape[0] // sources
    fetch = pltpu.make_async_copy(weight_ref.at[lax.axis_index("kv")], weight, sem)
    fetch.start()
    aux = part_ref[:, latent:].astype(jnp.float32)
    high = (aux[:, 0:1] + aux[:, 1:2] + aux[:, 2:3]).reshape(sources, requests, 1)
    denom = (aux[:, 3:4] + aux[:, 4:5] + aux[:, 5:6]).reshape(sources, requests, 1)
    factor = jnp.exp(high - jnp.max(high, axis=0, keepdims=True))
    total = jnp.sum(denom * factor, axis=0)
    parts = part_ref[:, :latent].astype(jnp.float32).reshape(sources, requests, latent)
    finished = jnp.sum(parts * factor, axis=0) / total
    rows = jnp.concatenate(parts_of(finished), axis=0).astype(jnp.bfloat16)
    fetch.wait()
    product = jnp.dot(rows, weight[...], preferred_element_type=jnp.float32)
    value = product[:requests] + product[requests : 2 * requests] + product[2 * requests :]
    value = jnp.concatenate([value] * copies, axis=0)
    out_ref[...] = value.astype(jnp.bfloat16)


def value_project(parts, w_uv, copies):
    heads, latent, value_width = w_uv.shape
    requests = parts.shape[0] // heads
    vmem = pl.BlockSpec(memory_space=pltpu.VMEM)
    return pl.pallas_call(
        functools.partial(value_kernel, copies),
        out_shape=jax.ShapeDtypeStruct((copies * requests, value_width), jnp.bfloat16),
        in_specs=[vmem, pl.BlockSpec(memory_space=pl.ANY)],
        out_specs=vmem,
        scratch_shapes=[
            pltpu.VMEM((latent, value_width), jnp.bfloat16),
            pltpu.SemaphoreType.DMA(()),
        ],
        compiler_params=pltpu.CompilerParams(vmem_limit_bytes=16 * MIB),
        name="value_project",
    )(parts, w_uv)


def body(queries, cache, slot_request, slot_page, lengths, w_uv, w_out, hidden):
    requests, heads, _ = queries.shape
    latent, value_width = w_uv.shape[1:]
    sections = lax.axis_size("section")
    sources = lax.axis_size("kv")
    groups = lax.axis_size("head")
    parts = attend(queries, cache, slot_request, slot_page, lengths, latent)
    parts = lax.all_to_all(parts, "kv", 0, 0, tiled=True)
    values = value_project(parts, w_uv, sections * sources)
    values = lax.all_to_all(values, ("section", "kv"), 0, 0, tiled=True)
    values = values.reshape(sections, sources, requests, value_width)
    values = values.transpose(0, 2, 1, 3).reshape(sections * requests, heads * value_width)
    projected = jnp.dot(values, w_out, preferred_element_type=jnp.float32)
    total = projected
    for step in (2, 1, 3):
        total = total + lax.ppermute(
            projected, "head", [(k, (k + step) % groups) for k in range(groups)]
        )
    return (hidden.astype(jnp.float32) + total).astype(jnp.bfloat16)


def solution(mesh):
    placed = (
        P("section", "head", None),
        P(("section", "kv"), None, None),
        P(("section", "kv")),
        P(("section", "kv")),
        P("section"),
        P("head", None, None),
        P("head", ("section", "kv")),
        P(None, ("section", "kv")),
    )
    return jax.shard_map(
        body, mesh=mesh, in_specs=placed, out_specs=P(None, ("section", "kv")), check_vma=False
    )
```

time: 257 us -> 72.2 us (0.28); the launches traced: 255 us -> 73.3 us
  waiting for transfers between devices: 68.2 us -> 2.36 us
  blocking collectives: 86.7 us -> 43 us
  local copies, waits for them, and re-layouts: 40.2 us -> 6.71 us
  matrix products: 22.6 us -> 0.34 us
  other arithmetic: 22.7 us -> 0.6 us
  Pallas kernels: 0 us -> 15.9 us
  between operations: 13.5 us -> 0.03 us
  starting transfers between devices: 0.01 us -> 4.4 us
    all_gather x3 -> x0, blocking collectives: 78.1 us -> none  [the longest x2 75.6 us: combined_all(): everything = jax.tree.map(lambda part: lax.all_gather(part, axis), array)]
    all_gather x1 -> x0, waiting for transfers between devices: 68.2 us -> none  [combined_all(): everything = jax.tree.map(lambda part: lax.all_gather(part, axis), array)]
    all_to_all x0 -> x2, blocking collectives: none -> 43 us  [the longest x1 24.1 us: body(): parts = lax.all_to_all(parts, 'kv', 0, 0, tiled=True)]
    dynamic_slice x31 -> x0, local copies, waits for them, and re-layouts: 33.6 us -> none  [lap(): return combine(so_far, jax.tree.map(lambda part: part[k], everything))]
    dot_general x6 -> x1, matrix products: 22.6 us -> 0.34 us  [body(): projected = jnp.dot(values, w_out, preferred_element_type=jnp.float32)]
    pallas_call x0 -> x2, Pallas kernels: none -> 15.9 us  [the longest x1 15.3 us: attend(): pl.pallas_call(attend_kernel, out_shape=jax.ShapeDtypeStruct((heads * req...]
    add x62 -> x0, other arithmetic: 13.1 us -> none  [the longest x31 12.5 us: combine(): summed_a * factor_a[..., None] + summed_b * factor_b[..., None]]
    psum x1 -> x0, blocking collectives: 8.55 us -> none  [body(): projected = lax.psum(projected, 'head')]
  transfers between devices with their start and end apart: 1 -> 3, of which waited for: 1 -> 2; matrix products, arithmetic and copies ran while one was open for 0% -> 0% of each run, Pallas kernels for 0% -> 0%
where the time goes in v1:
time: 72.2 us; the launch traced here: 73.3 us
  blocking collectives  43 us (60%)
  Pallas kernels  15.9 us (22%)
  local copies, waits for them, and re-layouts  6.71 us (9%)
  starting transfers between devices  4.4 us (6%)
  waiting for transfers between devices  2.36 us (3%)
    all_to_all x1, blocking collectives, body(): parts = lax.all_to_all(parts, 'kv', 0, 0, tiled=True)  24.1 us
    all_to_all x1, blocking collectives, body(): values = lax.all_to_all(values, ('section', 'kv'), 0, 0, tiled=True)  18.9 us
    pallas_call x1, Pallas kernels, attend(): pl.pallas_call(attend_kernel, out_shape=jax.ShapeDtypeStruct((heads * req...  15.3 us
    unnamed x16, local copies, waits for them, and re-layouts  6.71 us
    ppermute x3, starting transfers between devices, body(): lax.ppermute(projected, 'head', [(k, (k + step) % groups) for k in range(...  4.4 us
    ppermute x3, waiting for transfers between devices, body(): lax.ppermute(projected, 'head', [(k, (k + step) % groups) for k in range(...  2.36 us
  transfers between devices with their start and end apart: 3, of which 2 were waited for; matrix products, arithmetic and copies ran while one was open for 0% of the time, Pallas kernels for 0%

profile of v1, /device:TPU:1, one launch (start us, length us, event | category | flops | bytes accessed | tf_op | source)
XLA Modules:
  0.0 73.3 jit_solution(17179326653841035565)
XLA Ops:
  0.0 0.0 copy-start
  0.0 0.0 copy-start.1
  0.0 3.8 %copy-done.1 = bf16[64,128,576]{1,2,0:T(8,128)(2,1)S(1)} copy-done((bf16[64,128,576]{1,2,0:T(8,128)(2,1)S(1)}, bf16[64,128,576]{1,2,0:T(8,128)(2,1)}, u32[]{:S(2)}) %copy-start.1) | copy-done | bytes 9437208
  3.8 0.0 copy-start.3
  3.8 1.0 %copy-done.3 = bf16[8,32,576]{2,1,0:T(8,128)(2,1)S(1)} copy-done((bf16[8,32,576]{2,1,0:T(8,128)(2,1)S(1)}, bf16[8,32,576]{2,1,0:T(8,128)(2,1)}, u32[]{:S(2)}) %copy-start.3) | copy-done | bytes 294936
  4.7 0.0 copy-start.4
  4.7 0.7 copy-done.4
  5.4 0.0 copy-start.5
  5.4 0.7 copy-done.5
  6.0 0.0 copy-start.6
  6.1 0.7 copy-done.6
  6.7 0.0 copy-start.2
  6.7 0.0 copy-start.7
  6.7 15.3 %attend.1 = bf16[256,640]{1,0:T(8,128)(2,1)S(1)} custom-call(s32[64]{0:T(128)S(1)} %copy-done.4, s32[64]{0:T(128)S(1)} %copy-done.5, s32[8]{0:T(128)S(1)} %copy-done.6, bf16[8,32,576]{2,1,0:T(8,128)(2,1)S(1)} %copy-done.3, bf16[64,576,128]{2,1,0:T(8,128)(2,1)S(1)} %bitcast.11), custom_call_target="tpu_custom_call" | custom-call | tf_op jit(solution)/shard_map/attend/pallas_call | solution.py:120
  22.0 24.1 %all_to_all.20 = bf16[32,8,640]{2,1,0:T(8,128)(2,1)S(1)} all-to-all(bf16[32,8,640]{2,1,0:T(8,128)(2,1)S(1)} %bitcast.13), channel_id=1, replica_groups=mesh['section'=2,'kv'=32,'head'=4] {'kv'}, dimensions={0} | all-to-all | bytes 655360 | tf_op jit(solution)/shard_map/all_to_all | solution.py:188
  46.0 0.0 copy-done.2
  46.0 0.6 value_project.1
  46.7 18.9 %all_to_all.21 = bf16[64,8,128]{2,1,0:T(8,128)(2,1)S(1)} all-to-all(bf16[64,8,128]{2,1,0:T(8,128)(2,1)S(1)} %bitcast.14), channel_id=1, replica_groups=mesh['section'=2,'kv'=32,'head'=4] {'section','kv'}, dimensions={0} | all-to-all | bytes 262144 | tf_op jit(solution)/shard_map/all_to_all | solution.py:190
  65.6 0.0 copy-done
  65.6 0.3 fusion
  65.9 2.8 %collective-permute-start.2 = (f32[16,112]{1,0:T(8,128)S(1)}, f32[16,112]{1,0:T(8,128)S(1)}, u32[]{:S(2)}, u32[]{:S(2)}) collective-permute-start(f32[16,112]{1,0:T(8,128)S(1)} %fusion), channel_id=1, source_target_pairs={{0,3},{1,0},{2,1},{3,2},{4,7},{5,4},{6,5},{7,6},{8,11},{9,8},{10,9... | collective-permute-start | bytes 21512 | tf_op jit(solution)/shard_map/ppermute | solution.py:196
  68.7 0.0 collective-permute-start.1
  68.7 1.6 %collective-permute-start = (f32[16,112]{1,0:T(8,128)S(1)}, f32[16,112]{1,0:T(8,128)S(1)}, u32[]{:S(2)}, u32[]{:S(2)}) collective-permute-start(f32[16,112]{1,0:T(8,128)S(1)} %fusion), channel_id=1, source_target_pairs={{0,2},{1,3},{2,0},{3,1},{4,6},{5,7},{6,4},{7,5},{8,10},{9,11},{10,... | collective-permute-start | bytes 21512 | tf_op jit(solution)/shard_map/ppermute | solution.py:196
  70.3 0.0 collective-permute-done.2
  70.3 2.1 %collective-permute-done.1 = f32[16,112]{1,0:T(8,128)S(1)} collective-permute-done((f32[16,112]{1,0:T(8,128)S(1)}, f32[16,112]{1,0:T(8,128)S(1)}, u32[]{:S(2)}, u32[]{:S(2)}) %collective-permute-start.1) | collective-permute-done | bytes 7200 | tf_op jit(solution)/shard_map/ppermute | solution.py:196
  72.4 0.3 collective-permute-done
  72.7 0.0 copy-done.7
  72.7 0.6 add_convert_fusion
Async XLA Ops:
  0.0 65.6 %copy-start = (bf16[4096,112]{0,1:T(8,128)(2,1)S(1)}, bf16[4096,112]{0,1:T(8,128)(2,1)}, u32[]{:S(2)}) copy-start(bf16[4096,112]{0,1:T(8,128)(2,1)} %param.14) | copy-start | bytes 2752516
  0.0 3.8 %copy-start.1 = (bf16[64,128,576]{1,2,0:T(8,128)(2,1)S(1)}, bf16[64,128,576]{1,2,0:T(8,128)(2,1)}, u32[]{:S(2)}) copy-start(bf16[64,128,576]{1,2,0:T(8,128)(2,1)} %param.9) | copy-start | bytes 28311556
  3.8 1.0 %copy-start.3 = (bf16[8,32,576]{2,1,0:T(8,128)(2,1)S(1)}, bf16[8,32,576]{2,1,0:T(8,128)(2,1)}, u32[]{:S(2)}) copy-start(bf16[8,32,576]{2,1,0:T(8,128)(2,1)} %query_ref.1) | copy-start | bytes 884740
  4.7 0.7 copy-start.4
  5.4 0.7 copy-start.5
  6.0 0.7 copy-start.6
  6.7 39.3 %copy-start.2 = (bf16[32,512,128]{2,1,0:T(8,128)(2,1)S(1)}, bf16[32,512,128]{2,1,0:T(8,128)(2,1)}, u32[]{:S(2)}) copy-start(bf16[32,512,128]{2,1,0:T(8,128)(2,1)} %weight_ref.1) | copy-start | bytes 12582916
  6.7 66.0 %copy-start.7 = (bf16[16,112]{1,0:T(8,128)(2,1)S(1)}, bf16[16,112]{1,0:T(8,128)(2,1)}, u32[]{:S(2)}) copy-start(bf16[16,112]{1,0:T(8,128)(2,1)} %param.15) | copy-start | bytes 10756
  65.9 4.4 %collective-permute-start.2 = (f32[16,112]{1,0:T(8,128)S(1)}, f32[16,112]{1,0:T(8,128)S(1)}, u32[]{:S(2)}, u32[]{:S(2)}) collective-permute-start(f32[16,112]{1,0:T(8,128)S(1)} %fusion), channel_id=1, source_target_pairs={{0,3},{1,0},{2,1},{3,2},{4,7},{5,4},{6,5},{7,6},{8,11},{9,8},{10,9... | collective-permute-start | bytes 21512 | tf_op jit(solution)/shard_map/ppermute | solution.py:196
  68.7 3.7 %collective-permute-start.1 = (f32[16,112]{1,0:T(8,128)S(1)}, f32[16,112]{1,0:T(8,128)S(1)}, u32[]{:S(2)}, u32[]{:S(2)}) collective-permute-start(f32[16,112]{1,0:T(8,128)S(1)} %fusion), channel_id=1, source_target_pairs={{0,1},{1,2},{2,3},{3,0},{4,5},{5,6},{6,7},{7,4},{8,9},{9,10},{10,1... | collective-permute-start | bytes 21512 | tf_op jit(solution)/shard_map/ppermute | solution.py:196
  68.7 4.0 %collective-permute-start = (f32[16,112]{1,0:T(8,128)S(1)}, f32[16,112]{1,0:T(8,128)S(1)}, u32[]{:S(2)}, u32[]{:S(2)}) collective-permute-start(f32[16,112]{1,0:T(8,128)S(1)} %fusion), channel_id=1, source_target_pairs={{0,2},{1,3},{2,0},{3,1},{4,6},{5,7},{6,4},{7,5},{8,10},{9,11},{10,... | collective-permute-start | bytes 21512 | tf_op jit(solution)/shard_map/ppermute | solution.py:196

commit v2 on v1

--- a/solution.py
+++ b/solution.py
@@ -10,7 +10,9 @@
 ROPE = 64
 NOPE = 128
 LOWEST = -1e30
-UNROLL = 4
+UNROLL = 8
+AHEAD = 4
+SCAN = 16
 AUX = 128
 MIB = 1024 * 1024
 
@@ -23,79 +25,112 @@
 
 
 def attend_kernel(
-    owner_ref, page_ref, length_ref, query_ref, cache_ref, out_ref,
-    pages, scores, high, denom, summed, packed, slots, owners, counts, sems,
+    owner_hbm, page_hbm, length_hbm, query_hbm, cache_ref, out_ref,
+    pages, scores, high, denom, summed, packed, query_ref, owner_ref, page_ref, length_ref,
+    slots, sems, few,
 ):
     slot_count = cache_ref.shape[0]
     page_size = cache_ref.shape[2]
     requests, heads, _ = query_ref.shape
     latent = summed.shape[2]
     scale = (NOPE + ROPE) ** (-0.5)
-
-    def copy(slot):
-        return pltpu.make_async_copy(cache_ref.at[slot], pages.at[slot], sems.at[slot])
-
-    def find(slot, found):
-        owner = owner_ref[slot]
-
-        @pl.when(owner >= 0)
-        def _():
-            copy(slot).start()
-            mine = lax.rem(owner, requests)
-            slots[found] = slot
-            owners[found] = mine
-            counts[found] = length_ref[mine] - page_ref[slot] * page_size
-
-        return jnp.where(owner >= 0, found + 1, found)
-
-    live = lax.fori_loop(0, slot_count, find, jnp.int32(0))
-    blocks = lax.div(live + (UNROLL - 1), jnp.int32(UNROLL))
+    fetches = [
+        pltpu.make_async_copy(source, target, few.at[k])
+        for k, (source, target) in enumerate(
+            (
+                (owner_hbm, owner_ref),
+                (page_hbm, page_ref),
+                (length_hbm, length_ref),
+                (query_hbm, query_ref),
+            )
+        )
+    ]
+    for fetch in fetches:
+        fetch.start()
 
     high[...] = jnp.full(high.shape, LOWEST, jnp.float32)
     denom[...] = jnp.zeros(denom.shape, jnp.float32)
     summed[...] = jnp.zeros(summed.shape, jnp.float32)
+    for fetch in fetches[:3]:
+        fetch.wait()
+
+    def note(slot, found):
+        alive = owner_ref[slot] >= 0
+        slots[jnp.where(alive, found, slot_count - 1 - slot + found)] = slot
+        return jnp.where(alive, found + 1, found)
+
+    live = lax.fori_loop(0, slot_count, note, jnp.int32(0), unroll=SCAN)
+    blocks = lax.div(live + (UNROLL - 1), jnp.int32(UNROLL))
+
+    def fetch_block(block):
+        for k in range(UNROLL):
+            pltpu.make_async_copy(
+                cache_ref.at[slots[block * UNROLL + k]],
+                pages.at[block * UNROLL + k],
+                sems.at[block],
+            ).start()
+
+    def ahead(block, carry):
+        fetch_block(block)
+        return carry
+
+    lax.fori_loop(0, jnp.minimum(blocks, AHEAD), ahead, 0)
+
     column = lax.broadcasted_iota(jnp.int32, (heads, page_size), 1)
+
+    def entry_of(at):
+        slot = slots[at]
+        return slot, lax.rem(jnp.maximum(owner_ref[slot], 0), requests)
 
     def score(block, carry):
         first = block * UNROLL
-        for k in range(UNROLL):
-            @pl.when(first + k < live)
-            def _(k=k):
-                copy(slots[first + k]).wait()
-        for k in range(UNROLL):
-            at = first + k
-            entry = jnp.minimum(at, live - 1)
-            mine = owners[entry]
-            count = jnp.where(at < live, counts[entry], 0)
-            found = jnp.dot(
-                query_ref[mine], pages[slots[entry]], preferred_element_type=jnp.float32
-            ) * scale
-            found = jnp.where(column < count, found, LOWEST)
+
+        @pl.when(block + AHEAD < blocks)
+        def _():
+            fetch_block(block + AHEAD)
+
+        pltpu.make_async_copy(
+            cache_ref.at[pl.ds(0, UNROLL)], pages.at[pl.ds(first, UNROLL)], sems.at[block]
+        ).wait()
+
+        def keep(at, slot, mine, found):
+            count = jnp.where(at < live, length_ref[mine] - page_ref[slot] * page_size, 0)
+            found = jnp.where(column < count, found * scale, LOWEST)
             scores[at] = found
             high[mine] = jnp.maximum(high[mine], found)
+
+        for k in range(UNROLL):
+            slot, mine = entry_of(first + k)
+            keep(first + k, slot, mine, jnp.dot(
+                query_ref[mine], pages[first + k], preferred_element_type=jnp.float32
+            ))
         return carry
 
+    fetches[3].wait()
     lax.fori_loop(0, blocks, score, 0)
 
     for mine in range(requests):
         top = jnp.max(high[mine], axis=1, keepdims=True)
         high[mine] = jnp.broadcast_to(top, (heads, page_size))
 
+    def weigh(at):
+        slot, mine = entry_of(at)
+        weights = jnp.exp(scores[at] - high[mine])
+        weights = jnp.where(at < live, weights, 0.0)
+        denom[mine] += weights
+        return slot, mine, weights.astype(jnp.bfloat16)
+
     def gather(block, carry):
         first = block * UNROLL
-        for k in range(UNROLL):
-            at = first + k
-            entry = jnp.minimum(at, live - 1)
-            mine = owners[entry]
-            weights = jnp.exp(scores[at] - high[mine])
-            weights = jnp.where(at < live, weights, 0.0)
-            denom[mine] += weights
-            summed[mine] += lax.dot_general(
-                weights.astype(jnp.bfloat16),
-                pages[slots[entry], :latent, :],
-                (((1,), (1,)), ((), ())),
-                preferred_element_type=jnp.float32,
-            )
+        for k in range(0, UNROLL, 2):
+            sa, ma, wa = weigh(first + k)
+            sb, mb, wb = weigh(first + k + 1)
+            zero = jnp.zeros_like(wa)
+            lhs = jnp.concatenate([jnp.concatenate([wa, zero], axis=1), jnp.concatenate([zero, wb], axis=1)], axis=0)
+            rhs = jnp.concatenate([pages[first + k, :latent, :], pages[first + k + 1, :latent, :]], axis=1)
+            both = lax.dot_general(lhs, rhs, (((1,), (1,)), ((), ())), preferred_element_type=jnp.float32)
+            summed[ma] += both[:heads]
+            summed[mb] += both[heads:]
         return carry
 
     lax.fori_loop(0, blocks, gather, 0)
@@ -115,12 +150,11 @@
     requests, heads, width = queries.shape
     slot_count, page_size, _ = cache.shape
     padded = slot_count + UNROLL
-    smem = pl.BlockSpec(memory_space=pltpu.SMEM)
     vmem = pl.BlockSpec(memory_space=pltpu.VMEM)
     return pl.pallas_call(
         attend_kernel,
         out_shape=jax.ShapeDtypeStruct((heads * requests, latent + AUX), jnp.bfloat16),
-        in_specs=[smem, smem, smem, vmem, pl.BlockSpec(memory_space=pl.ANY)],
+        in_specs=[pl.BlockSpec(memory_space=pltpu.HBM)] * 5,
         out_specs=vmem,
         scratch_shapes=[
             pltpu.VMEM((slot_count, width, page_size), jnp.bfloat16),
@@ -129,12 +163,15 @@
             pltpu.VMEM((requests, heads, page_size), jnp.float32),
             pltpu.VMEM((requests, heads, latent), jnp.float32),
             pltpu.VMEM((heads, requests, latent + AUX), jnp.float32),
+            pltpu.VMEM(queries.shape, queries.dtype),
+            pltpu.SMEM(slot_request.shape, jnp.int32),
+            pltpu.SMEM(slot_page.shape, jnp.int32),
+            pltpu.SMEM(lengths.shape, jnp.int32),
             pltpu.SMEM((padded,), jnp.int32),
-            pltpu.SMEM((padded,), jnp.int32),
-            pltpu.SMEM((padded,), jnp.int32),
-            pltpu.SemaphoreType.DMA((slot_count,)),
+            pltpu.SemaphoreType.DMA((slot_count // UNROLL,)),
+            pltpu.SemaphoreType.DMA((4,)),
         ],
-        compiler_params=pltpu.CompilerParams(vmem_limit_bytes=40 * MIB),
+        compiler_params=pltpu.CompilerParams(vmem_limit_bytes=62 * MIB),
         name="attend",
     )(slot_request, slot_page, lengths, queries, jnp.swapaxes(cache, 1, 2))
 
@@ -173,7 +210,7 @@
             pltpu.VMEM((latent, value_width), jnp.bfloat16),
             pltpu.SemaphoreType.DMA(()),
         ],
-        compiler_params=pltpu.CompilerParams(vmem_limit_bytes=16 * MIB),
+        compiler_params=pltpu.CompilerParams(vmem_limit_bytes=61 * MIB),
         name="value_project",
     )(parts, w_uv)
 

time: 72.2 us -> 60.6 us (0.84); the launches traced: 73.3 us -> 59.8 us
  local copies, waits for them, and re-layouts: 6.71 us -> 0.01 us
  Pallas kernels: 15.9 us -> 9.48 us
    pallas_call x1, Pallas kernels: 15.3 us -> 6.8 us  [attend(): pl.pallas_call(attend_kernel, out_shape=jax.ShapeDtypeStruct((heads * req...]
    unnamed x16 -> x4, local copies, waits for them, and re-layouts: 6.71 us -> 0.01 us
    pallas_call x1, Pallas kernels: 0.6 us -> 2.69 us  [value_project(): pl.pallas_call(functools.partial(value_kernel, copies), out_shape=jax.Sha...]
    all_to_all x1, blocking collectives: 24.1 us -> 23.1 us  [body(): parts = lax.all_to_all(parts, 'kv', 0, 0, tiled=True)]
where the time goes in v2:
time: 60.6 us; the launch traced here: 59.8 us
  blocking collectives  42.6 us (70%)
  Pallas kernels  9.48 us (16%)
  starting transfers between devices  4.4 us (7%)
  waiting for transfers between devices  2.36 us (4%)
    all_to_all x1, blocking collectives, body(): parts = lax.all_to_all(parts, 'kv', 0, 0, tiled=True)  23.1 us
    all_to_all x1, blocking collectives, body(): values = lax.all_to_all(values, ('section', 'kv'), 0, 0, tiled=True)  19.5 us
    pallas_call x1, Pallas kernels, attend(): pl.pallas_call(attend_kernel, out_shape=jax.ShapeDtypeStruct((heads * req...  6.8 us
    ppermute x3, starting transfers between devices, body(): lax.ppermute(projected, 'head', [(k, (k + step) % groups) for k in range(...  4.4 us
    pallas_call x1, Pallas kernels, value_project(): pl.pallas_call(functools.partial(value_kernel, copies), out_shape=jax.Sha...  2.69 us
    ppermute x3, waiting for transfers between devices, body(): lax.ppermute(projected, 'head', [(k, (k + step) % groups) for k in range(...  2.36 us
  transfers between devices with their start and end apart: 3, of which 2 were waited for; matrix products, arithmetic and copies ran while one was open for 0% of the time, Pallas kernels for 0%

profile of v2, /device:TPU:1, one launch (start us, length us, event | category | flops | bytes accessed | tf_op | source)
XLA Modules:
  0.0 59.8 jit_solution(16854463252046251460)
XLA Ops:
  0.0 0.0 copy-start
  0.0 0.0 copy-start.1
  0.0 6.8 %attend.1 = bf16[256,640]{1,0:T(8,128)(2,1)} custom-call(s32[64]{0:T(128)} %owner_hbm.1, s32[64]{0:T(128)} %page_hbm.1, s32[8]{0:T(128)} %length_hbm.1, bf16[8,32,576]{2,1,0:T(8,128)(2,1)} %query_hbm.1, bf16[64,576,128]{2,1,0:T(8,128)(2,1)} %bitcast.11), custom_call_target="tpu_custom_call" | custom-call | tf_op jit(solution)/shard_map/attend/pallas_call | solution.py:154
  6.8 23.1 %all_to_all.20 = bf16[32,8,640]{2,1,0:T(8,128)(2,1)} all-to-all(bf16[32,8,640]{2,1,0:T(8,128)(2,1)} %bitcast.13), channel_id=1, replica_groups=mesh['section'=2,'kv'=32,'head'=4] {'kv'}, dimensions={0} | all-to-all | bytes 655360 | tf_op jit(solution)/shard_map/all_to_all | solution.py:225
  29.9 2.7 %value_project.1 = bf16[512,128]{1,0:T(8,128)(2,1)} custom-call(bf16[256,640]{1,0:T(8,128)(2,1)} %bitcast.12, bf16[32,512,128]{2,1,0:T(8,128)(2,1)} %weight_ref.1), custom_call_target="tpu_custom_call" | custom-call | tf_op jit(solution)/shard_map/value_project/pallas_call | solution.py:204
  32.6 19.5 %all_to_all.21 = bf16[64,8,128]{2,1,0:T(8,128)(2,1)S(1)} all-to-all(bf16[64,8,128]{2,1,0:T(8,128)(2,1)} %bitcast.14), channel_id=1, replica_groups=mesh['section'=2,'kv'=32,'head'=4] {'section','kv'}, dimensions={0} | all-to-all | bytes 262144 | tf_op jit(solution)/shard_map/all_to_all | solution.py:227
  52.1 0.0 copy-done
  52.1 0.3 fusion
  52.4 2.8 %collective-permute-start.2 = (f32[16,112]{1,0:T(8,128)S(1)}, f32[16,112]{1,0:T(8,128)S(1)}, u32[]{:S(2)}, u32[]{:S(2)}) collective-permute-start(f32[16,112]{1,0:T(8,128)S(1)} %fusion), channel_id=1, source_target_pairs={{0,3},{1,0},{2,1},{3,2},{4,7},{5,4},{6,5},{7,6},{8,11},{9,8},{10,9... | collective-permute-start | bytes 21512 | tf_op jit(solution)/shard_map/ppermute | solution.py:233
  55.2 0.0 collective-permute-start.1
  55.2 1.6 %collective-permute-start = (f32[16,112]{1,0:T(8,128)S(1)}, f32[16,112]{1,0:T(8,128)S(1)}, u32[]{:S(2)}, u32[]{:S(2)}) collective-permute-start(f32[16,112]{1,0:T(8,128)S(1)} %fusion), channel_id=1, source_target_pairs={{0,2},{1,3},{2,0},{3,1},{4,6},{5,7},{6,4},{7,5},{8,10},{9,11},{10,... | collective-permute-start | bytes 21512 | tf_op jit(solution)/shard_map/ppermute | solution.py:233
  56.8 0.0 collective-permute-done.2
  56.8 2.1 %collective-permute-done.1 = f32[16,112]{1,0:T(8,128)S(1)} collective-permute-done((f32[16,112]{1,0:T(8,128)S(1)}, f32[16,112]{1,0:T(8,128)S(1)}, u32[]{:S(2)}, u32[]{:S(2)}) %collective-permute-start.1) | collective-permute-done | bytes 7200 | tf_op jit(solution)/shard_map/ppermute | solution.py:233
  58.9 0.3 collective-permute-done
  59.2 0.0 copy-done.1
  59.2 0.6 %add_convert_fusion = bf16[16,112]{1,0:T(8,128)(2,1)} fusion(f32[16,112]{1,0:T(8,128)S(1)} %collective-permute-done.2, f32[16,112]{1,0:T(8,128)S(1)} %collective-permute-done.1, f32[16,112]{1,0:T(8,128)S(1)} %fusion, f32[16,112]{1,0:T(8,128)S(1)} %collective-permute-done, bf16[16,112]{1,0:T(8,128)(2,1)S(1)} %copy-done.1), kind=kLoop, calls=%fused_computation | loop fusion | flops 10752 | bytes 35840 | tf_op jit(solution)/shard_map/convert_element_type | solution.py:236
Async XLA Ops:
  0.0 52.1 %copy-start = (bf16[4096,112]{0,1:T(8,128)(2,1)S(1)}, bf16[4096,112]{0,1:T(8,128)(2,1)}, u32[]{:S(2)}) copy-start(bf16[4096,112]{0,1:T(8,128)(2,1)} %param.14) | copy-start | bytes 2752516
  0.0 59.2 %copy-start.1 = (bf16[16,112]{1,0:T(8,128)(2,1)S(1)}, bf16[16,112]{1,0:T(8,128)(2,1)}, u32[]{:S(2)}) copy-start(bf16[16,112]{1,0:T(8,128)(2,1)} %param.15) | copy-start | bytes 10756
  52.4 4.4 %collective-permute-start.2 = (f32[16,112]{1,0:T(8,128)S(1)}, f32[16,112]{1,0:T(8,128)S(1)}, u32[]{:S(2)}, u32[]{:S(2)}) collective-permute-start(f32[16,112]{1,0:T(8,128)S(1)} %fusion), channel_id=1, source_target_pairs={{0,3},{1,0},{2,1},{3,2},{4,7},{5,4},{6,5},{7,6},{8,11},{9,8},{10,9... | collective-permute-start | bytes 21512 | tf_op jit(solution)/shard_map/ppermute | solution.py:233
  55.2 3.7 %collective-permute-start.1 = (f32[16,112]{1,0:T(8,128)S(1)}, f32[16,112]{1,0:T(8,128)S(1)}, u32[]{:S(2)}, u32[]{:S(2)}) collective-permute-start(f32[16,112]{1,0:T(8,128)S(1)} %fusion), channel_id=1, source_target_pairs={{0,1},{1,2},{2,3},{3,0},{4,5},{5,6},{6,7},{7,4},{8,9},{9,10},{10,1... | collective-permute-start | bytes 21512 | tf_op jit(solution)/shard_map/ppermute | solution.py:233
  55.2 4.0 %collective-permute-start = (f32[16,112]{1,0:T(8,128)S(1)}, f32[16,112]{1,0:T(8,128)S(1)}, u32[]{:S(2)}, u32[]{:S(2)}) collective-permute-start(f32[16,112]{1,0:T(8,128)S(1)} %fusion), channel_id=1, source_target_pairs={{0,2},{1,3},{2,0},{3,1},{4,6},{5,7},{6,4},{7,5},{8,10},{9,11},{10,... | collective-permute-start | bytes 21512 | tf_op jit(solution)/shard_map/ppermute | solution.py:233

commit v3 on v2

v3 whole, which is shorter than its diff:
```python
import functools

import jax
import jax.numpy as jnp
from jax import lax
from jax.experimental import pallas as pl
from jax.experimental.pallas import tpu as pltpu
from jax.sharding import PartitionSpec as P

ROPE = 64
NOPE = 128
LOWEST = -1e30
UNROLL = 8
AHEAD = 4
SCAN = 16
BLIND = 16
AUX = 128
MIB = 1024 * 1024


def parts_of(value):
    high = value.astype(jnp.bfloat16).astype(jnp.float32)
    rest = value - high
    middle = rest.astype(jnp.bfloat16).astype(jnp.float32)
    return high, middle, rest - middle


def attend_kernel(
    owner_hbm, page_hbm, length_hbm, query_hbm, cache_ref, weight_hbm, out_ref, weight_ref,
    pages, scores, high, denom, summed, packed, query_ref, owner_ref, page_ref, length_ref,
    slots, sems, few,
):
    slot_count = cache_ref.shape[0]
    page_size = cache_ref.shape[2]
    requests, heads, _ = query_ref.shape
    latent = summed.shape[2]
    scale = (NOPE + ROPE) ** (-0.5)
    fetches = [
        pltpu.make_async_copy(source, target, few.at[k])
        for k, (source, target) in enumerate(
            (
                (owner_hbm, owner_ref),
                (page_hbm, page_ref),
                (length_hbm, length_ref),
                (query_hbm, query_ref),
                (weight_hbm.at[lax.axis_index("kv")], weight_ref),
            )
        )
    ]
    for fetch in fetches:
        fetch.start()

    def blind(part):
        span = pl.ds(part * UNROLL, UNROLL)
        return pltpu.make_async_copy(cache_ref.at[span], pages.at[span], sems.at[part])

    early = BLIND // UNROLL
    for part in range(early):
        blind(part).start()

    high[...] = jnp.full(high.shape, LOWEST, jnp.float32)
    denom[...] = jnp.zeros(denom.shape, jnp.float32)
    summed[...] = jnp.zeros(summed.shape, jnp.float32)
    for fetch in fetches[:3]:
        fetch.wait()

    def note(slot, found):
        alive = owner_ref[slot] >= 0
        slots[jnp.where(alive, found, slot_count - 1 - slot + found)] = slot
        return jnp.where(alive, found + 1, found)

    for k in range(UNROLL):
        slots[slot_count + k] = 0
    here = lax.fori_loop(0, BLIND, note, jnp.int32(0), unroll=SCAN)
    live = lax.fori_loop(BLIND, slot_count, note, here, unroll=SCAN)
    blocks = lax.div(live + (UNROLL - 1), jnp.int32(UNROLL))
    batches = lax.div(live - here + (UNROLL - 1), jnp.int32(UNROLL))

    def fetch_batch(batch):
        for k in range(UNROLL):
            pltpu.make_async_copy(
                cache_ref.at[slots[here + batch * UNROLL + k]],
                pages.at[BLIND + batch * UNROLL + k],
                sems.at[early + batch],
            ).start()

    def ahead(batch, carry):
        fetch_batch(batch)
        return carry

    lax.fori_loop(0, jnp.minimum(batches, AHEAD), ahead, 0)

    column = lax.broadcasted_iota(jnp.int32, (heads, page_size), 1)

    def entry_of(at):
        slot = slots[at]
        place = jnp.where(at < here, slot, BLIND - here + at)
        place = jnp.where(at < live, place, 0)
        return slot, place, lax.rem(jnp.maximum(owner_ref[slot], 0), requests)

    def arrive(batch, carry):
        @pl.when(batch + AHEAD < batches)
        def _():
            fetch_batch(batch + AHEAD)

        span = pl.ds(BLIND + batch * UNROLL, UNROLL)
        pltpu.make_async_copy(
            cache_ref.at[pl.ds(0, UNROLL)], pages.at[span], sems.at[early + batch]
        ).wait()
        return carry

    def score(block, arrived):
        first = block * UNROLL
        needed = lax.div(first + (2 * UNROLL - 1) - here, jnp.int32(UNROLL))
        needed = jnp.clip(needed, arrived, batches)
        lax.fori_loop(arrived, needed, arrive, 0)

        def keep(at, slot, mine, found):
            count = jnp.where(at < live, length_ref[mine] - page_ref[slot] * page_size, 0)
            found = jnp.where(column < count, found * scale, LOWEST)
            scores[at] = found
            high[mine] = jnp.maximum(high[mine], found)

        for k in range(UNROLL):
            slot, place, mine = entry_of(first + k)
            keep(first + k, slot, mine, jnp.dot(
                query_ref[mine], pages[place], preferred_element_type=jnp.float32
            ))
        return needed

    fetches[3].wait()
    for part in range(early):
        blind(part).wait()
    lax.fori_loop(0, blocks, score, jnp.int32(0))

    for mine in range(requests):
        top = jnp.max(high[mine], axis=1, keepdims=True)
        high[mine] = jnp.broadcast_to(top, (heads, page_size))

    def weigh(at):
        slot, place, mine = entry_of(at)
        weights = jnp.exp(scores[at] - high[mine])
        weights = jnp.where(at < live, weights, 0.0)
        denom[mine] += weights
        return place, mine, weights.astype(jnp.bfloat16)

    def gather(block, carry):
        first = block * UNROLL
        for k in range(0, UNROLL, 2):
            sa, ma, wa = weigh(first + k)
            sb, mb, wb = weigh(first + k + 1)
            zero = jnp.zeros_like(wa)
            lhs = jnp.concatenate([jnp.concatenate([wa, zero], axis=1), jnp.concatenate([zero, wb], axis=1)], axis=0)
            rhs = jnp.concatenate([pages[sa, :latent, :], pages[sb, :latent, :]], axis=1)
            both = lax.dot_general(lhs, rhs, (((1,), (1,)), ((), ())), preferred_element_type=jnp.float32)
            summed[ma] += both[:heads]
            summed[mb] += both[heads:]
        return carry

    lax.fori_loop(0, blocks, gather, 0)

    lane = lax.broadcasted_iota(jnp.int32, (heads, AUX), 1)
    for mine in range(requests):
        packed[:, mine, :latent] = summed[mine]
        total = jnp.broadcast_to(jnp.sum(denom[mine], axis=1, keepdims=True), (heads, AUX))
        aux = jnp.zeros((heads, AUX), jnp.float32)
        for k, part in enumerate(parts_of(high[mine]) + parts_of(total)):
            aux = jnp.where(lane == k, part, aux)
        packed[:, mine, latent:] = aux
    fetches[4].wait()
    out_ref[...] = packed[...].reshape(out_ref.shape).astype(jnp.bfloat16)


def attend(queries, cache, slot_request, slot_page, lengths, w_uv):
    requests, heads, width = queries.shape
    slot_count, page_size, _ = cache.shape
    padded = slot_count + UNROLL
    latent = w_uv.shape[1]
    operands = (slot_request, slot_page, lengths, queries, jnp.swapaxes(cache, 1, 2), w_uv)
    operands = [pltpu.with_memory_space_constraint(k, pltpu.HBM) for k in operands]
    vmem = pl.BlockSpec(memory_space=pltpu.VMEM)
    return pl.pallas_call(
        attend_kernel,
        out_shape=(
            jax.ShapeDtypeStruct((heads * requests, latent + AUX), jnp.bfloat16),
            jax.ShapeDtypeStruct(w_uv.shape[1:], w_uv.dtype),
        ),
        in_specs=[pl.BlockSpec(memory_space=pltpu.HBM)] * len(operands),
        out_specs=(vmem, vmem),
        scratch_shapes=[
            pltpu.VMEM((slot_count, width, page_size), jnp.bfloat16),
            pltpu.VMEM((padded, heads, page_size), jnp.float32),
            pltpu.VMEM((requests, heads, page_size), jnp.float32),
            pltpu.VMEM((requests, heads, page_size), jnp.float32),
            pltpu.VMEM((requests, heads, latent), jnp.float32),
            pltpu.VMEM((heads, requests, latent + AUX), jnp.float32),
            pltpu.VMEM(queries.shape, queries.dtype),
            pltpu.SMEM(slot_request.shape, jnp.int32),
            pltpu.SMEM(slot_page.shape, jnp.int32),
            pltpu.SMEM(lengths.shape, jnp.int32),
            pltpu.SMEM((padded,), jnp.int32),
            pltpu.SemaphoreType.DMA((padded // UNROLL,)),
            pltpu.SemaphoreType.DMA((len(operands) - 1,)),
        ],
        compiler_params=pltpu.CompilerParams(vmem_limit_bytes=24 * MIB),
        name="attend",
    )(*operands)


def value_kernel(copies, part_ref, weight_ref, out_ref):
    latent = weight_ref.shape[0]
    requests = out_ref.shape[0] // copies
    sources = part_ref.shape[0] // requests
    aux = part_ref[:, latent:].astype(jnp.float32)
    high = (aux[:, 0:1] + aux[:, 1:2] + aux[:, 2:3]).reshape(sources, requests, 1)
    denom = (aux[:, 3:4] + aux[:, 4:5] + aux[:, 5:6]).reshape(sources, requests, 1)
    factor = jnp.exp(high - jnp.max(high, axis=0, keepdims=True))
    total = jnp.sum(denom * factor, axis=0)
    parts = part_ref[:, :latent].astype(jnp.float32).reshape(sources, requests, latent)
    finished = jnp.sum(parts * factor, axis=0) / total
    rows = jnp.concatenate(parts_of(finished), axis=0).astype(jnp.bfloat16)
    product = jnp.dot(rows, weight_ref[...], preferred_element_type=jnp.float32)
    value = product[:requests] + product[requests : 2 * requests] + product[2 * requests :]
    value = jnp.concatenate([value] * copies, axis=0)
    out_ref[...] = value.astype(jnp.bfloat16)


def value_project(parts, weight, requests, copies):
    vmem = pl.BlockSpec(memory_space=pltpu.VMEM)
    return pl.pallas_call(
        functools.partial(value_kernel, copies),
        out_shape=jax.ShapeDtypeStruct((copies * requests, weight.shape[1]), jnp.bfloat16),
        in_specs=[vmem, vmem],
        out_specs=vmem,
        compiler_params=pltpu.CompilerParams(vmem_limit_bytes=16 * MIB),
        name="value_project",
    )(parts, weight)


def body(queries, cache, slot_request, slot_page, lengths, w_uv, w_out, hidden):
    requests, heads, _ = queries.shape
    value_width = w_uv.shape[2]
    sections = lax.axis_size("section")
    sources = lax.axis_size("kv")
    groups = lax.axis_size("head")
    parts, weight = attend(queries, cache, slot_request, slot_page, lengths, w_uv)
    parts = lax.all_to_all(parts, "kv", 0, 0, tiled=True)
    values = value_project(parts, weight, requests, sections * sources)
    values = lax.all_to_all(values, ("section", "kv"), 0, 0, tiled=True)
    values = values.reshape(sections, sources, requests, value_width)
    values = values.transpose(0, 2, 1, 3).reshape(sections * requests, heads * value_width)
    projected = jnp.dot(values, w_out, preferred_element_type=jnp.float32)
    total = projected
    for step in (2, 1, 3):
        total = total + lax.ppermute(
            projected, "head", [(k, (k + step) % groups) for k in range(groups)]
        )
    return (hidden.astype(jnp.float32) + total).astype(jnp.bfloat16)


def solution(mesh):
    placed = (
        P("section", "head", None),
        P(("section", "kv"), None, None),
        P(("section", "kv")),
        P(("section", "kv")),
        P("section"),
        P("head", None, None),
        P("head", ("section", "kv")),
        P(None, ("section", "kv")),
    )
    return jax.shard_map(
        body, mesh=mesh, in_specs=placed, out_specs=P(None, ("section", "kv")), check_vma=False
    )
```

time: 60.6 us -> 57.2 us (0.944); the launches traced: 59.8 us -> 57.1 us
  Pallas kernels: 9.48 us -> 7.2 us
    all_to_all x1, blocking collectives: 19.5 us -> 17.1 us  [body(): values = lax.all_to_all(values, ('section', 'kv'), 0, 0, tiled=True)]
    pallas_call x1, Pallas kernels: 2.69 us -> 0.42 us  [value_project(): pl.pallas_call(functools.partial(value_kernel, copies), out_shape=jax.Sha...]
    all_to_all x1, blocking collectives: 23.1 us -> 25 us  [body(): parts = lax.all_to_all(parts, 'kv', 0, 0, tiled=True)]
where the time goes in v3:
time: 57.2 us; the launch traced here: 57.1 us
  blocking collectives  42.1 us (74%)
  Pallas kernels  7.2 us (13%)
  starting transfers between devices  4.4 us (8%)
  waiting for transfers between devices  2.36 us (4%)
  other arithmetic  0.6 us (1%)
    all_to_all x1, blocking collectives, body(): parts = lax.all_to_all(parts, 'kv', 0, 0, tiled=True)  25 us
    all_to_all x1, blocking collectives, body(): values = lax.all_to_all(values, ('section', 'kv'), 0, 0, tiled=True)  17.1 us
    pallas_call x1, Pallas kernels, attend(): pl.pallas_call(attend_kernel, out_shape=(jax.ShapeDtypeStruct((heads * re...  6.78 us
    ppermute x3, starting transfers between devices, body(): lax.ppermute(projected, 'head', [(k, (k + step) % groups) for k in range(...  4.4 us
    ppermute x3, waiting for transfers between devices, body(): lax.ppermute(projected, 'head', [(k, (k + step) % groups) for k in range(...  2.36 us
  transfers between devices with their start and end apart: 3, of which 2 were waited for; matrix products, arithmetic and copies ran while one was open for 0% of the time, Pallas kernels for 0%

profile of v3, /device:TPU:1, one launch (start us, length us, event | category | flops | bytes accessed | tf_op | source)
XLA Modules:
  0.0 57.1 jit_solution(13055367112358748259)
XLA Ops:
  0.0 0.0 copy-start
  0.0 0.0 copy-start.1
  0.0 6.8 %attend.1 = (bf16[256,640]{1,0:T(8,128)(2,1)S(1)}, bf16[512,128]{1,0:T(8,128)(2,1)S(1)}) custom-call(s32[64]{0:T(128)} %owner_hbm.1, s32[64]{0:T(128)} %page_hbm.1, s32[8]{0:T(128)} %length_hbm.1, bf16[8,32,576]{2,1,0:T(8,128)(2,1)} %query_hbm.1, bf16[64,576,128]{2,1,0:T(8,128)(2,1)} %bitcast.14, bf16[32,512,128]{2,1,0:T(8,128)(2,1)} %weight_hbm.1), custom_call_target="tpu_custom_call" | custom-call | tf_op jit(solution)/shard_map/attend/pallas_call | solution.py:182
  6.8 25.0 %all_to_all.20 = bf16[32,8,640]{2,1,0:T(8,128)(2,1)S(1)} all-to-all(bf16[32,8,640]{2,1,0:T(8,128)(2,1)S(1)} %bitcast.13), channel_id=1, replica_groups=mesh['section'=2,'kv'=32,'head'=4] {'kv'}, dimensions={0} | all-to-all | bytes 655360 | tf_op jit(solution)/shard_map/all_to_all | solution.py:247
  31.8 0.4 value_project.1
  32.2 17.1 %all_to_all.21 = bf16[64,8,128]{2,1,0:T(8,128)(2,1)S(1)} all-to-all(bf16[64,8,128]{2,1,0:T(8,128)(2,1)S(1)} %bitcast.12), channel_id=1, replica_groups=mesh['section'=2,'kv'=32,'head'=4] {'section','kv'}, dimensions={0} | all-to-all | bytes 262144 | tf_op jit(solution)/shard_map/all_to_all | solution.py:249
  49.4 0.0 copy-done
  49.4 0.3 fusion
  49.7 2.8 %collective-permute-start.2 = (f32[16,112]{1,0:T(8,128)S(1)}, f32[16,112]{1,0:T(8,128)S(1)}, u32[]{:S(2)}, u32[]{:S(2)}) collective-permute-start(f32[16,112]{1,0:T(8,128)S(1)} %fusion), channel_id=1, source_target_pairs={{0,3},{1,0},{2,1},{3,2},{4,7},{5,4},{6,5},{7,6},{8,11},{9,8},{10,9... | collective-permute-start | bytes 21512 | tf_op jit(solution)/shard_map/ppermute | solution.py:255
  52.4 0.0 collective-permute-start.1
  52.5 1.6 %collective-permute-start = (f32[16,112]{1,0:T(8,128)S(1)}, f32[16,112]{1,0:T(8,128)S(1)}, u32[]{:S(2)}, u32[]{:S(2)}) collective-permute-start(f32[16,112]{1,0:T(8,128)S(1)} %fusion), channel_id=1, source_target_pairs={{0,2},{1,3},{2,0},{3,1},{4,6},{5,7},{6,4},{7,5},{8,10},{9,11},{10,... | collective-permute-start | bytes 21512 | tf_op jit(solution)/shard_map/ppermute | solution.py:255
  54.1 0.0 collective-permute-done.2
  54.1 2.1 %collective-permute-done.1 = f32[16,112]{1,0:T(8,128)S(1)} collective-permute-done((f32[16,112]{1,0:T(8,128)S(1)}, f32[16,112]{1,0:T(8,128)S(1)}, u32[]{:S(2)}, u32[]{:S(2)}) %collective-permute-start.1) | collective-permute-done | bytes 7200 | tf_op jit(solution)/shard_map/ppermute | solution.py:255
  56.2 0.3 collective-permute-done
  56.5 0.0 copy-done.1
  56.5 0.6 %add_convert_fusion = bf16[16,112]{1,0:T(8,128)(2,1)} fusion(f32[16,112]{1,0:T(8,128)S(1)} %collective-permute-done.2, f32[16,112]{1,0:T(8,128)S(1)} %collective-permute-done.1, f32[16,112]{1,0:T(8,128)S(1)} %fusion, f32[16,112]{1,0:T(8,128)S(1)} %collective-permute-done, bf16[16,112]{1,0:T(8,128)(2,1)S(1)} %copy-done.1), kind=kLoop, calls=%fused_computation | loop fusion | flops 10752 | bytes 35840 | tf_op jit(solution)/shard_map/convert_element_type | solution.py:258
Async XLA Ops:
  0.0 49.4 %copy-start = (bf16[4096,112]{0,1:T(8,128)(2,1)S(1)}, bf16[4096,112]{0,1:T(8,128)(2,1)}, u32[]{:S(2)}) copy-start(bf16[4096,112]{0,1:T(8,128)(2,1)} %param.14) | copy-start | bytes 2752516
  0.0 56.5 %copy-start.1 = (bf16[16,112]{1,0:T(8,128)(2,1)S(1)}, bf16[16,112]{1,0:T(8,128)(2,1)}, u32[]{:S(2)}) copy-start(bf16[16,112]{1,0:T(8,128)(2,1)} %param.15) | copy-start | bytes 10756
  49.7 4.4 %collective-permute-start.2 = (f32[16,112]{1,0:T(8,128)S(1)}, f32[16,112]{1,0:T(8,128)S(1)}, u32[]{:S(2)}, u32[]{:S(2)}) collective-permute-start(f32[16,112]{1,0:T(8,128)S(1)} %fusion), channel_id=1, source_target_pairs={{0,3},{1,0},{2,1},{3,2},{4,7},{5,4},{6,5},{7,6},{8,11},{9,8},{10,9... | collective-permute-start | bytes 21512 | tf_op jit(solution)/shard_map/ppermute | solution.py:255
  52.4 3.7 %collective-permute-start.1 = (f32[16,112]{1,0:T(8,128)S(1)}, f32[16,112]{1,0:T(8,128)S(1)}, u32[]{:S(2)}, u32[]{:S(2)}) collective-permute-start(f32[16,112]{1,0:T(8,128)S(1)} %fusion), channel_id=1, source_target_pairs={{0,1},{1,2},{2,3},{3,0},{4,5},{5,6},{6,7},{7,4},{8,9},{9,10},{10,1... | collective-permute-start | bytes 21512 | tf_op jit(solution)/shard_map/ppermute | solution.py:255
  52.5 4.0 %collective-permute-start = (f32[16,112]{1,0:T(8,128)S(1)}, f32[16,112]{1,0:T(8,128)S(1)}, u32[]{:S(2)}, u32[]{:S(2)}) collective-permute-start(f32[16,112]{1,0:T(8,128)S(1)} %fusion), channel_id=1, source_target_pairs={{0,2},{1,3},{2,0},{3,1},{4,6},{5,7},{6,4},{7,5},{8,10},{9,11},{10,... | collective-permute-start | bytes 21512 | tf_op jit(solution)/shard_map/ppermute | solution.py:255

commit v4 on v3

--- a/solution.py
+++ b/solution.py
@@ -14,6 +14,7 @@
 AHEAD = 4
 SCAN = 16
 BLIND = 16
+GROUP = 16
 AUX = 128
 MIB = 1024 * 1024
 
@@ -26,9 +27,9 @@
 
 
 def attend_kernel(
-    owner_hbm, page_hbm, length_hbm, query_hbm, cache_ref, weight_hbm, out_ref, weight_ref,
-    pages, scores, high, denom, summed, packed, query_ref, owner_ref, page_ref, length_ref,
-    slots, sems, few,
+    owner_hbm, page_hbm, length_hbm, query_hbm, cache_ref, weight_hbm, out_ref,
+    pages, scores, high, denom, summed, packed, values, query_ref, owner_ref, page_ref, length_ref,
+    weight_ref, slots, sems, few,
 ):
     slot_count = cache_ref.shape[0]
     page_size = cache_ref.shape[2]
@@ -43,11 +44,11 @@
                 (page_hbm, page_ref),
                 (length_hbm, length_ref),
                 (query_hbm, query_ref),
-                (weight_hbm.at[lax.axis_index("kv")], weight_ref),
+                (weight_hbm, weight_ref),
             )
         )
     ]
-    for fetch in fetches:
+    for fetch in fetches[:4]:
         fetch.start()
 
     def blind(part):
@@ -132,6 +133,7 @@
     for part in range(early):
         blind(part).wait()
     lax.fori_loop(0, blocks, score, jnp.int32(0))
+    fetches[4].start()
 
     for mine in range(requests):
         top = jnp.max(high[mine], axis=1, keepdims=True)
@@ -160,15 +162,28 @@
     lax.fori_loop(0, blocks, gather, 0)
 
     lane = lax.broadcasted_iota(jnp.int32, (heads, AUX), 1)
+    width = weight_ref.shape[2]
     for mine in range(requests):
-        packed[:, mine, :latent] = summed[mine]
+        packed[:, mine, :] = summed[mine]
         total = jnp.broadcast_to(jnp.sum(denom[mine], axis=1, keepdims=True), (heads, AUX))
         aux = jnp.zeros((heads, AUX), jnp.float32)
         for k, part in enumerate(parts_of(high[mine]) + parts_of(total)):
             aux = jnp.where(lane == k, part, aux)
-        packed[:, mine, latent:] = aux
+        values[:, mine, width:] = aux
     fetches[4].wait()
-    out_ref[...] = packed[...].reshape(out_ref.shape).astype(jnp.bfloat16)
+
+    def project(block, carry):
+        for k in range(GROUP):
+            head = block * GROUP + k
+            rows = jnp.concatenate(parts_of(packed[head]), axis=0).astype(jnp.bfloat16)
+            product = jnp.dot(rows, weight_ref[head], preferred_element_type=jnp.float32)
+            values[head, :, :width] = (
+                product[:requests] + product[requests : 2 * requests] + product[2 * requests :]
+            )
+        return carry
+
+    lax.fori_loop(0, heads // GROUP, project, 0)
+    out_ref[...] = values[...].reshape(out_ref.shape).astype(jnp.bfloat16)
 
 
 def attend(queries, cache, slot_request, slot_page, lengths, w_uv):
@@ -181,60 +196,56 @@
     vmem = pl.BlockSpec(memory_space=pltpu.VMEM)
     return pl.pallas_call(
         attend_kernel,
-        out_shape=(
-            jax.ShapeDtypeStruct((heads * requests, latent + AUX), jnp.bfloat16),
-            jax.ShapeDtypeStruct(w_uv.shape[1:], w_uv.dtype),
-        ),
+        out_shape=jax.ShapeDtypeStruct((heads * requests, w_uv.shape[2] + AUX), jnp.bfloat16),
         in_specs=[pl.BlockSpec(memory_space=pltpu.HBM)] * len(operands),
-        out_specs=(vmem, vmem),
+        out_specs=vmem,
         scratch_shapes=[
             pltpu.VMEM((slot_count, width, page_size), jnp.bfloat16),
             pltpu.VMEM((padded, heads, page_size), jnp.float32),
             pltpu.VMEM((requests, heads, page_size), jnp.float32),
             pltpu.VMEM((requests, heads, page_size), jnp.float32),
             pltpu.VMEM((requests, heads, latent), jnp.float32),
-            pltpu.VMEM((heads, requests, latent + AUX), jnp.float32),
+            pltpu.VMEM((heads, requests, latent), jnp.float32),
+            pltpu.VMEM((heads, requests, w_uv.shape[2] + AUX), jnp.float32),
             pltpu.VMEM(queries.shape, queries.dtype),
             pltpu.SMEM(slot_request.shape, jnp.int32),
             pltpu.SMEM(slot_page.shape, jnp.int32),
             pltpu.SMEM(lengths.shape, jnp.int32),
+            pltpu.VMEM(w_uv.shape, w_uv.dtype),
             pltpu.SMEM((padded,), jnp.int32),
             pltpu.SemaphoreType.DMA((padded // UNROLL,)),
             pltpu.SemaphoreType.DMA((len(operands) - 1,)),
         ],
-        compiler_params=pltpu.CompilerParams(vmem_limit_bytes=24 * MIB),
+        compiler_params=pltpu.CompilerParams(vmem_limit_bytes=28 * MIB),
         name="attend",
     )(*operands)
 
 
-def value_kernel(copies, part_ref, weight_ref, out_ref):
-    latent = weight_ref.shape[0]
+def combine_kernel(copies, part_ref, out_ref):
+    width = out_ref.shape[1]
     requests = out_ref.shape[0] // copies
     sources = part_ref.shape[0] // requests
-    aux = part_ref[:, latent:].astype(jnp.float32)
+    aux = part_ref[:, width:].astype(jnp.float32)
     high = (aux[:, 0:1] + aux[:, 1:2] + aux[:, 2:3]).reshape(sources, requests, 1)
     denom = (aux[:, 3:4] + aux[:, 4:5] + aux[:, 5:6]).reshape(sources, requests, 1)
     factor = jnp.exp(high - jnp.max(high, axis=0, keepdims=True))
     total = jnp.sum(denom * factor, axis=0)
-    parts = part_ref[:, :latent].astype(jnp.float32).reshape(sources, requests, latent)
-    finished = jnp.sum(parts * factor, axis=0) / total
-    rows = jnp.concatenate(parts_of(finished), axis=0).astype(jnp.bfloat16)
-    product = jnp.dot(rows, weight_ref[...], preferred_element_type=jnp.float32)
-    value = product[:requests] + product[requests : 2 * requests] + product[2 * requests :]
+    parts = part_ref[:, :width].astype(jnp.float32).reshape(sources, requests, width)
+    value = jnp.sum(parts * factor, axis=0) / total
     value = jnp.concatenate([value] * copies, axis=0)
     out_ref[...] = value.astype(jnp.bfloat16)
 
 
-def value_project(parts, weight, requests, copies):
+def combine(parts, requests, width, copies):
     vmem = pl.BlockSpec(memory_space=pltpu.VMEM)
     return pl.pallas_call(
-        functools.partial(value_kernel, copies),
-        out_shape=jax.ShapeDtypeStruct((copies * requests, weight.shape[1]), jnp.bfloat16),
-        in_specs=[vmem, vmem],
+        functools.partial(combine_kernel, copies),
+        out_shape=jax.ShapeDtypeStruct((copies * requests, width), jnp.bfloat16),
+        in_specs=[vmem],
         out_specs=vmem,
         compiler_params=pltpu.CompilerParams(vmem_limit_bytes=16 * MIB),
-        name="value_project",
-    )(parts, weight)
+        name="combine",
+    )(parts)
 
 
 def body(queries, cache, slot_request, slot_page, lengths, w_uv, w_out, hidden):
@@ -243,9 +254,9 @@
     sections = lax.axis_size("section")
     sources = lax.axis_size("kv")
     groups = lax.axis_size("head")
-    parts, weight = attend(queries, cache, slot_request, slot_page, lengths, w_uv)
+    parts = attend(queries, cache, slot_request, slot_page, lengths, w_uv)
     parts = lax.all_to_all(parts, "kv", 0, 0, tiled=True)
-    values = value_project(parts, weight, requests, sections * sources)
+    values = combine(parts, requests, value_width, sections * sources)
     values = lax.all_to_all(values, ("section", "kv"), 0, 0, tiled=True)
     values = values.reshape(sections, sources, requests, value_width)
     values = values.transpose(0, 2, 1, 3).reshape(sections * requests, heads * value_width)

time: 57.2 us -> 54.2 us (0.948)
  blocking collectives: 42.1 us -> 38.5 us
  Pallas kernels: 7.2 us -> 7.83 us
    all_to_all x1, blocking collectives: 25 us -> 20.9 us  [body(): parts = lax.all_to_all(parts, 'kv', 0, 0, tiled=True)]
    pallas_call x2, Pallas kernels: 7.2 us -> 7.83 us  [the longest x1 7.53 us: attend(): pl.pallas_call(attend_kernel, out_shape=jax.ShapeDtypeStruct((heads * req...]
where the time goes in v4:
time: 54.2 us; the launch traced here: 54 us
  blocking collectives  38.5 us (71%)
  Pallas kernels  7.83 us (14%)
  starting transfers between devices  4.39 us (8%)
  waiting for transfers between devices  2.36 us (4%)
  other arithmetic  0.6 us (1%)
    all_to_all x1, blocking collectives, body(): parts = lax.all_to_all(parts, 'kv', 0, 0, tiled=True)  20.9 us
    all_to_all x1, blocking collectives, body(): values = lax.all_to_all(values, ('section', 'kv'), 0, 0, tiled=True)  17.5 us
    pallas_call x1, Pallas kernels, attend(): pl.pallas_call(attend_kernel, out_shape=jax.ShapeDtypeStruct((heads * req...  7.53 us
    ppermute x3, starting transfers between devices, body(): lax.ppermute(projected, 'head', [(k, (k + step) % groups) for k in range(...  4.39 us
    ppermute x3, waiting for transfers between devices, body(): lax.ppermute(projected, 'head', [(k, (k + step) % groups) for k in range(...  2.36 us
  transfers between devices with their start and end apart: 3, of which 2 were waited for; matrix products, arithmetic and copies ran while one was open for 0% of the time, Pallas kernels for 0%

profile of v4, /device:TPU:1, one launch (start us, length us, event | category | flops | bytes accessed | tf_op | source)
XLA Modules:
  0.0 54.0 jit_solution(16569589266743810062)
XLA Ops:
  0.0 0.0 copy-start
  0.0 0.0 copy-start.1
  0.0 7.5 %attend.1 = bf16[256,256]{1,0:T(8,128)(2,1)S(1)} custom-call(s32[64]{0:T(128)} %owner_hbm.1, s32[64]{0:T(128)} %page_hbm.1, s32[8]{0:T(128)} %length_hbm.1, bf16[8,32,576]{2,1,0:T(8,128)(2,1)} %query_hbm.1, bf16[64,576,128]{2,1,0:T(8,128)(2,1)} %bitcast.14, bf16[32,512,128]{2,1,0:T(8,128)(2,1)} %weight_hbm.1), custom_call_target="tpu_custom_call" | custom-call | tf_op jit(solution)/shard_map/attend/pallas_call | solution.py:197
  7.5 20.9 %all_to_all.20 = bf16[32,8,256]{2,1,0:T(8,128)(2,1)S(1)} all-to-all(bf16[32,8,256]{2,1,0:T(8,128)(2,1)S(1)} %bitcast.11), channel_id=1, replica_groups=mesh['section'=2,'kv'=32,'head'=4] {'kv'}, dimensions={0} | all-to-all | bytes 262144 | tf_op jit(solution)/shard_map/all_to_all | solution.py:258
  28.5 0.3 combine.1
  28.8 17.5 %all_to_all.21 = bf16[64,8,128]{2,1,0:T(8,128)(2,1)S(1)} all-to-all(bf16[64,8,128]{2,1,0:T(8,128)(2,1)S(1)} %bitcast.13), channel_id=1, replica_groups=mesh['section'=2,'kv'=32,'head'=4] {'section','kv'}, dimensions={0} | all-to-all | bytes 262144 | tf_op jit(solution)/shard_map/all_to_all | solution.py:260
  46.3 0.0 copy-done
  46.3 0.3 fusion
  46.7 2.7 %collective-permute-start.2 = (f32[16,112]{1,0:T(8,128)S(1)}, f32[16,112]{1,0:T(8,128)S(1)}, u32[]{:S(2)}, u32[]{:S(2)}) collective-permute-start(f32[16,112]{1,0:T(8,128)S(1)} %fusion), channel_id=1, source_target_pairs={{0,3},{1,0},{2,1},{3,2},{4,7},{5,4},{6,5},{7,6},{8,11},{9,8},{10,9... | collective-permute-start | bytes 21512 | tf_op jit(solution)/shard_map/ppermute | solution.py:266
  49.4 0.0 collective-permute-start.1
  49.4 1.6 %collective-permute-start = (f32[16,112]{1,0:T(8,128)S(1)}, f32[16,112]{1,0:T(8,128)S(1)}, u32[]{:S(2)}, u32[]{:S(2)}) collective-permute-start(f32[16,112]{1,0:T(8,128)S(1)} %fusion), channel_id=1, source_target_pairs={{0,2},{1,3},{2,0},{3,1},{4,6},{5,7},{6,4},{7,5},{8,10},{9,11},{10,... | collective-permute-start | bytes 21512 | tf_op jit(solution)/shard_map/ppermute | solution.py:266
  51.1 0.0 collective-permute-done.2
  51.1 2.1 %collective-permute-done.1 = f32[16,112]{1,0:T(8,128)S(1)} collective-permute-done((f32[16,112]{1,0:T(8,128)S(1)}, f32[16,112]{1,0:T(8,128)S(1)}, u32[]{:S(2)}, u32[]{:S(2)}) %collective-permute-start.1) | collective-permute-done | bytes 7200 | tf_op jit(solution)/shard_map/ppermute | solution.py:266
  53.1 0.3 collective-permute-done
  53.4 0.0 copy-done.1
  53.4 0.6 %add_convert_fusion = bf16[16,112]{1,0:T(8,128)(2,1)} fusion(f32[16,112]{1,0:T(8,128)S(1)} %collective-permute-done.2, f32[16,112]{1,0:T(8,128)S(1)} %collective-permute-done.1, f32[16,112]{1,0:T(8,128)S(1)} %fusion, f32[16,112]{1,0:T(8,128)S(1)} %collective-permute-done, bf16[16,112]{1,0:T(8,128)(2,1)S(1)} %copy-done.1), kind=kLoop, calls=%fused_computation | loop fusion | flops 10752 | bytes 35840 | tf_op jit(solution)/shard_map/convert_element_type | solution.py:269
Async XLA Ops:
  0.0 46.3 %copy-start = (bf16[4096,112]{0,1:T(8,128)(2,1)S(1)}, bf16[4096,112]{0,1:T(8,128)(2,1)}, u32[]{:S(2)}) copy-start(bf16[4096,112]{0,1:T(8,128)(2,1)} %param.14) | copy-start | bytes 2752516
  0.0 53.4 %copy-start.1 = (bf16[16,112]{1,0:T(8,128)(2,1)S(1)}, bf16[16,112]{1,0:T(8,128)(2,1)}, u32[]{:S(2)}) copy-start(bf16[16,112]{1,0:T(8,128)(2,1)} %param.15) | copy-start | bytes 10756
  46.7 4.4 %collective-permute-start.2 = (f32[16,112]{1,0:T(8,128)S(1)}, f32[16,112]{1,0:T(8,128)S(1)}, u32[]{:S(2)}, u32[]{:S(2)}) collective-permute-start(f32[16,112]{1,0:T(8,128)S(1)} %fusion), channel_id=1, source_target_pairs={{0,3},{1,0},{2,1},{3,2},{4,7},{5,4},{6,5},{7,6},{8,11},{9,8},{10,9... | collective-permute-start | bytes 21512 | tf_op jit(solution)/shard_map/ppermute | solution.py:266
  49.4 3.7 %collective-permute-start.1 = (f32[16,112]{1,0:T(8,128)S(1)}, f32[16,112]{1,0:T(8,128)S(1)}, u32[]{:S(2)}, u32[]{:S(2)}) collective-permute-start(f32[16,112]{1,0:T(8,128)S(1)} %fusion), channel_id=1, source_target_pairs={{0,1},{1,2},{2,3},{3,0},{4,5},{5,6},{6,7},{7,4},{8,9},{9,10},{10,1... | collective-permute-start | bytes 21512 | tf_op jit(solution)/shard_map/ppermute | solution.py:266
  49.4 4.0 %collective-permute-start = (f32[16,112]{1,0:T(8,128)S(1)}, f32[16,112]{1,0:T(8,128)S(1)}, u32[]{:S(2)}, u32[]{:S(2)}) collective-permute-start(f32[16,112]{1,0:T(8,128)S(1)} %fusion), channel_id=1, source_target_pairs={{0,2},{1,3},{2,0},{3,1},{4,6},{5,7},{6,4},{7,5},{8,10},{9,11},{10,... | collective-permute-start | bytes 21512 | tf_op jit(solution)/shard_map/ppermute | solution.py:266

commit v5 on v4

--- a/solution.py
+++ b/solution.py
@@ -256,16 +256,19 @@
     groups = lax.axis_size("head")
     parts = attend(queries, cache, slot_request, slot_page, lengths, w_uv)
     parts = lax.all_to_all(parts, "kv", 0, 0, tiled=True)
-    values = combine(parts, requests, value_width, sections * sources)
-    values = lax.all_to_all(values, ("section", "kv"), 0, 0, tiled=True)
-    values = values.reshape(sections, sources, requests, value_width)
+    values = combine(parts, requests, value_width, sources)
+    values = lax.all_to_all(values, "kv", 0, 0, tiled=True)
+    others = lax.ppermute(values, "section", [(0, 1), (1, 0)])
+    values = jnp.stack([values, others]).reshape(sections, sources, requests, value_width)
     values = values.transpose(0, 2, 1, 3).reshape(sections * requests, heads * value_width)
     projected = jnp.dot(values, w_out, preferred_element_type=jnp.float32)
     total = projected
-    for step in (2, 1, 3):
+    for step in (1, 3, 2):
         total = total + lax.ppermute(
             projected, "head", [(k, (k + step) % groups) for k in range(groups)]
         )
+    swapped = jnp.concatenate([total[requests:], total[:requests]])
+    total = jnp.where(lax.axis_index("section") == 0, total, swapped)
     return (hidden.astype(jnp.float32) + total).astype(jnp.bfloat16)
 
 

time: 54.2 us -> 53.9 us (level)
  blocking collectives: 38.5 us -> 34.5 us
  starting transfers between devices: 4.39 us -> 7.06 us
  waiting for transfers between devices: 2.36 us -> 3.31 us
    all_to_all x1, blocking collectives: 17.5 us -> 12.1 us  [body(): values = lax.all_to_all(values, 'kv', 0, 0, tiled=True)]
    ppermute x0 -> x1, starting transfers between devices: none -> 2.66 us  [body(): others = lax.ppermute(values, 'section', [(0, 1), (1, 0)])]
    all_to_all x1, blocking collectives: 20.9 us -> 22.4 us  [body(): parts = lax.all_to_all(parts, 'kv', 0, 0, tiled=True)]
    ppermute x0 -> x1, waiting for transfers between devices: none -> 0.9 us  [body(): others = lax.ppermute(values, 'section', [(0, 1), (1, 0)])]
  transfers between devices with their start and end apart: 3 -> 4, of which waited for: 2 -> 2; matrix products, arithmetic and copies ran while one was open for 0% -> 0% of each run, Pallas kernels for 0% -> 0%
where the time goes in v5:
time: 53.9 us; the launch traced here: 53.7 us
  blocking collectives  34.5 us (64%)
  Pallas kernels  7.83 us (15%)
  starting transfers between devices  7.06 us (13%)
  waiting for transfers between devices  3.31 us (6%)
  other arithmetic  0.61 us (1%)
    all_to_all x1, blocking collectives, body(): parts = lax.all_to_all(parts, 'kv', 0, 0, tiled=True)  22.4 us
    all_to_all x1, blocking collectives, body(): values = lax.all_to_all(values, 'kv', 0, 0, tiled=True)  12.1 us
    pallas_call x1, Pallas kernels, attend(): pl.pallas_call(attend_kernel, out_shape=jax.ShapeDtypeStruct((heads * req...  7.53 us
    ppermute x3, starting transfers between devices, body(): lax.ppermute(projected, 'head', [(k, (k + step) % groups) for k in range(...  4.39 us
    ppermute x1, starting transfers between devices, body(): others = lax.ppermute(values, 'section', [(0, 1), (1, 0)])  2.66 us
    ppermute x3, waiting for transfers between devices, body(): lax.ppermute(projected, 'head', [(k, (k + step) % groups) for k in range(...  2.41 us
  transfers between devices with their start and end apart: 4, of which 2 were waited for; matrix products, arithmetic and copies ran while one was open for 0% of the time, Pallas kernels for 0%

profile of v5, /device:TPU:1, one launch (start us, length us, event | category | flops | bytes accessed | tf_op | source)
XLA Modules:
  0.0 53.7 jit_solution(2381408148701301468)
XLA Ops:
  0.0 0.0 copy-start
  0.0 0.0 copy-start.1
  0.0 7.5 %attend.1 = bf16[256,256]{1,0:T(8,128)(2,1)S(1)} custom-call(s32[64]{0:T(128)} %owner_hbm.1, s32[64]{0:T(128)} %page_hbm.1, s32[8]{0:T(128)} %length_hbm.1, bf16[8,32,576]{2,1,0:T(8,128)(2,1)} %query_hbm.1, bf16[64,576,128]{2,1,0:T(8,128)(2,1)} %bitcast.16, bf16[32,512,128]{2,1,0:T(8,128)(2,1)} %weight_hbm.1), custom_call_target="tpu_custom_call" | custom-call | tf_op jit(solution)/shard_map/attend/pallas_call | solution.py:197
  7.5 22.4 %all_to_all.23 = bf16[32,8,256]{2,1,0:T(8,128)(2,1)S(1)} all-to-all(bf16[32,8,256]{2,1,0:T(8,128)(2,1)S(1)} %bitcast.13), channel_id=1, replica_groups=mesh['section'=2,'kv'=32,'head'=4] {'kv'}, dimensions={0} | all-to-all | bytes 262144 | tf_op jit(solution)/shard_map/all_to_all | solution.py:258
  29.9 0.3 combine.1
  30.2 12.1 %all_to_all.24 = bf16[32,8,128]{2,1,0:T(8,128)(2,1)S(1)} all-to-all(bf16[32,8,128]{2,1,0:T(8,128)(2,1)S(1)} %bitcast.15), channel_id=1, replica_groups=mesh['section'=2,'kv'=32,'head'=4] {'kv'}, dimensions={0} | all-to-all | bytes 131072 | tf_op jit(solution)/shard_map/all_to_all | solution.py:260
  42.4 2.7 %collective-permute-start = (bf16[256,128]{1,0:T(8,128)(2,1)S(1)}, bf16[256,128]{1,0:T(8,128)(2,1)S(1)}, u32[]{:S(2)}, u32[]{:S(2)}) collective-permute-start(bf16[256,128]{1,0:T(8,128)(2,1)S(1)} %bitcast.17), channel_id=1, source_target_pairs={{0,128},{128,0},{1,129},{129,1},{2,130},{130,2},{3,131},{131,3},{4... | collective-permute-start | bytes 196616 | tf_op jit(solution)/shard_map/ppermute | solution.py:261
  45.0 0.9 %collective-permute-done = bf16[256,128]{1,0:T(8,128)(2,1)S(1)} collective-permute-done((bf16[256,128]{1,0:T(8,128)(2,1)S(1)}, bf16[256,128]{1,0:T(8,128)(2,1)S(1)}, u32[]{:S(2)}, u32[]{:S(2)}) %collective-permute-start) | collective-permute-done | bytes 65568 | tf_op jit(solution)/shard_map/ppermute | solution.py:261
  45.9 0.0 copy-done
  45.9 0.3 fusion
  46.3 1.3 %collective-permute-start.1 = (f32[16,112]{1,0:T(8,128)S(1)}, f32[16,112]{1,0:T(8,128)S(1)}, u32[]{:S(2)}, u32[]{:S(2)}) collective-permute-start(f32[16,112]{1,0:T(8,128)S(1)} %fusion), channel_id=1, source_target_pairs={{0,1},{1,2},{2,3},{3,0},{4,5},{5,6},{6,7},{7,4},{8,9},{9,10},{10,1... | collective-permute-start | bytes 21512 | tf_op jit(solution)/shard_map/ppermute | solution.py:267
  47.6 1.5 %collective-permute-start.2 = (f32[16,112]{1,0:T(8,128)S(1)}, f32[16,112]{1,0:T(8,128)S(1)}, u32[]{:S(2)}, u32[]{:S(2)}) collective-permute-start(f32[16,112]{1,0:T(8,128)S(1)} %fusion), channel_id=1, source_target_pairs={{0,3},{1,0},{2,1},{3,2},{4,7},{5,4},{6,5},{7,6},{8,11},{9,8},{10,9... | collective-permute-start | bytes 21512 | tf_op jit(solution)/shard_map/ppermute | solution.py:267
  49.1 1.6 %collective-permute-start.3 = (f32[16,112]{1,0:T(8,128)S(1)}, f32[16,112]{1,0:T(8,128)S(1)}, u32[]{:S(2)}, u32[]{:S(2)}) collective-permute-start(f32[16,112]{1,0:T(8,128)S(1)} %fusion), channel_id=1, source_target_pairs={{0,2},{1,3},{2,0},{3,1},{4,6},{5,7},{6,4},{7,5},{8,10},{9,11},{10,... | collective-permute-start | bytes 21512 | tf_op jit(solution)/shard_map/ppermute | solution.py:267
  50.7 0.0 collective-permute-done.1
  50.7 0.0 collective-permute-done.2
  50.7 2.4 %collective-permute-done.3 = f32[16,112]{1,0:T(8,128)S(1)} collective-permute-done((f32[16,112]{1,0:T(8,128)S(1)}, f32[16,112]{1,0:T(8,128)S(1)}, u32[]{:S(2)}, u32[]{:S(2)}) %collective-permute-start.3) | collective-permute-done | bytes 7200 | tf_op jit(solution)/shard_map/ppermute | solution.py:267
  53.1 0.0 copy-done.1
  53.1 0.6 %fusion.4 = bf16[16,112]{1,0:T(8,128)(2,1)} fusion(f32[16,112]{1,0:T(8,128)S(1)} %add_add_fusion, f32[8,112]{1,0:T(8,128)S(1)} %get-tuple-element.6, f32[8,112]{1,0:T(8,128)S(1)} %get-tuple-element.5, bf16[16,112]{1,0:T(8,128)(2,1)S(1)} %copy-done.1, pred[]{:T(512)S(6)} %eq.3), kind=kLoop, calls=%fused_computation.6 | loop fusion | flops 8960 | bytes 21505 | tf_op jit(solution)/shard_map/convert_element_type | solution.py:272
  (2 shorter events, 0.0 us)
Async XLA Ops:
  0.0 45.9 %copy-start = (bf16[4096,112]{0,1:T(8,128)(2,1)S(1)}, bf16[4096,112]{0,1:T(8,128)(2,1)}, u32[]{:S(2)}) copy-start(bf16[4096,112]{0,1:T(8,128)(2,1)} %param.14) | copy-start | bytes 2752516
  0.0 53.1 %copy-start.1 = (bf16[16,112]{1,0:T(8,128)(2,1)S(1)}, bf16[16,112]{1,0:T(8,128)(2,1)}, u32[]{:S(2)}) copy-start(bf16[16,112]{1,0:T(8,128)(2,1)} %param.15) | copy-start | bytes 10756
  42.4 3.6 %collective-permute-start = (bf16[256,128]{1,0:T(8,128)(2,1)S(1)}, bf16[256,128]{1,0:T(8,128)(2,1)S(1)}, u32[]{:S(2)}, u32[]{:S(2)}) collective-permute-start(bf16[256,128]{1,0:T(8,128)(2,1)S(1)} %bitcast.17), channel_id=1, source_target_pairs={{0,128},{128,0},{1,129},{129,1},{2,130},{130,2},{3,131},{131,3},{4... | collective-permute-start | bytes 196616 | tf_op jit(solution)/shard_map/ppermute | solution.py:261
  46.3 4.4 %collective-permute-start.1 = (f32[16,112]{1,0:T(8,128)S(1)}, f32[16,112]{1,0:T(8,128)S(1)}, u32[]{:S(2)}, u32[]{:S(2)}) collective-permute-start(f32[16,112]{1,0:T(8,128)S(1)} %fusion), channel_id=1, source_target_pairs={{0,1},{1,2},{2,3},{3,0},{4,5},{5,6},{6,7},{7,4},{8,9},{9,10},{10,1... | collective-permute-start | bytes 21512 | tf_op jit(solution)/shard_map/ppermute | solution.py:267
  47.6 3.1 %collective-permute-start.2 = (f32[16,112]{1,0:T(8,128)S(1)}, f32[16,112]{1,0:T(8,128)S(1)}, u32[]{:S(2)}, u32[]{:S(2)}) collective-permute-start(f32[16,112]{1,0:T(8,128)S(1)} %fusion), channel_id=1, source_target_pairs={{0,3},{1,0},{2,1},{3,2},{4,7},{5,4},{6,5},{7,6},{8,11},{9,8},{10,9... | collective-permute-start | bytes 21512 | tf_op jit(solution)/shard_map/ppermute | solution.py:267
  49.1 4.0 %collective-permute-start.3 = (f32[16,112]{1,0:T(8,128)S(1)}, f32[16,112]{1,0:T(8,128)S(1)}, u32[]{:S(2)}, u32[]{:S(2)}) collective-permute-start(f32[16,112]{1,0:T(8,128)S(1)} %fusion), channel_id=1, source_target_pairs={{0,2},{1,3},{2,0},{3,1},{4,6},{5,7},{6,4},{7,5},{8,10},{9,11},{10,... | collective-permute-start | bytes 21512 | tf_op jit(solution)/shard_map/ppermute | solution.py:267

commit v6 on v5

--- a/solution.py
+++ b/solution.py
@@ -12,9 +12,10 @@
 LOWEST = -1e30
 UNROLL = 8
 AHEAD = 4
+WIDE = 2
 SCAN = 16
 BLIND = 16
-GROUP = 16
+GROUP = 32
 AUX = 128
 MIB = 1024 * 1024
 
@@ -110,9 +111,8 @@
         ).wait()
         return carry
 
-    def score(block, arrived):
-        first = block * UNROLL
-        needed = lax.div(first + (2 * UNROLL - 1) - here, jnp.int32(UNROLL))
+    def score(span, first, arrived):
+        needed = lax.div(first + (span + UNROLL - 1) - here, jnp.int32(UNROLL))
         needed = jnp.clip(needed, arrived, batches)
         lax.fori_loop(arrived, needed, arrive, 0)
 
@@ -122,7 +122,7 @@
             scores[at] = found
             high[mine] = jnp.maximum(high[mine], found)
 
-        for k in range(UNROLL):
+        for k in range(span):
             slot, place, mine = entry_of(first + k)
             keep(first + k, slot, mine, jnp.dot(
                 query_ref[mine], pages[place], preferred_element_type=jnp.float32
@@ -132,7 +132,16 @@
     fetches[3].wait()
     for part in range(early):
         blind(part).wait()
-    lax.fori_loop(0, blocks, score, jnp.int32(0))
+
+    def sweep(step, carry):
+        wide = lax.div(blocks, jnp.int32(WIDE))
+        span = WIDE * UNROLL
+        carry = lax.fori_loop(0, wide, lambda k, c: step(span, k * span, c), carry)
+        return lax.fori_loop(
+            wide * WIDE, blocks, lambda k, c: step(UNROLL, k * UNROLL, c), carry
+        )
+
+    sweep(score, jnp.int32(0))
     fetches[4].start()
 
     for mine in range(requests):
@@ -146,9 +155,8 @@
         denom[mine] += weights
         return place, mine, weights.astype(jnp.bfloat16)
 
-    def gather(block, carry):
-        first = block * UNROLL
-        for k in range(0, UNROLL, 2):
+    def gather(span, first, carry):
+        for k in range(0, span, 2):
             sa, ma, wa = weigh(first + k)
             sb, mb, wb = weigh(first + k + 1)
             zero = jnp.zeros_like(wa)
@@ -159,7 +167,7 @@
             summed[mb] += both[heads:]
         return carry
 
-    lax.fori_loop(0, blocks, gather, 0)
+    sweep(gather, 0)
 
     lane = lax.broadcasted_iota(jnp.int32, (heads, AUX), 1)
     width = weight_ref.shape[2]

time: 53.9 us -> 53.7 us (level)
  Pallas kernels: 7.83 us -> 8.94 us
  starting transfers between devices: 7.06 us -> 6.02 us
    pallas_call x1, Pallas kernels: 7.53 us -> 8.65 us  [attend(): pl.pallas_call(attend_kernel, out_shape=jax.ShapeDtypeStruct((heads * req...]
    ppermute x1, starting transfers between devices: 2.66 us -> 1.62 us  [body(): others = lax.ppermute(values, 'section', [(0, 1), (1, 0)])]
where the time goes in v6:
time: 53.7 us; the launch traced here: 53.3 us
  blocking collectives  34 us (63%)
  Pallas kernels  8.94 us (17%)
  starting transfers between devices  6.02 us (11%)
  waiting for transfers between devices  3.31 us (6%)
  other arithmetic  0.61 us (1%)
    all_to_all x1, blocking collectives, body(): parts = lax.all_to_all(parts, 'kv', 0, 0, tiled=True)  22.2 us
    all_to_all x1, blocking collectives, body(): values = lax.all_to_all(values, 'kv', 0, 0, tiled=True)  11.8 us
    pallas_call x1, Pallas kernels, attend(): pl.pallas_call(attend_kernel, out_shape=jax.ShapeDtypeStruct((heads * req...  8.65 us
    ppermute x3, starting transfers between devices, body(): lax.ppermute(projected, 'head', [(k, (k + step) % groups) for k in range(...  4.4 us
    ppermute x3, waiting for transfers between devices, body(): lax.ppermute(projected, 'head', [(k, (k + step) % groups) for k in range(...  2.41 us
    ppermute x1, starting transfers between devices, body(): others = lax.ppermute(values, 'section', [(0, 1), (1, 0)])  1.62 us
  transfers between devices with their start and end apart: 4, of which 2 were waited for; matrix products, arithmetic and copies ran while one was open for 0% of the time, Pallas kernels for 0%

profile of v6, /device:TPU:1, one launch (start us, length us, event | category | flops | bytes accessed | tf_op | source)
XLA Modules:
  0.0 53.3 jit_solution(4876065417392205014)
XLA Ops:
  0.0 0.0 copy-start
  0.0 0.0 copy-start.1
  0.0 8.6 %attend.1 = bf16[256,256]{1,0:T(8,128)(2,1)S(1)} custom-call(s32[64]{0:T(128)} %owner_hbm.1, s32[64]{0:T(128)} %page_hbm.1, s32[8]{0:T(128)} %length_hbm.1, bf16[8,32,576]{2,1,0:T(8,128)(2,1)} %query_hbm.1, bf16[64,576,128]{2,1,0:T(8,128)(2,1)} %bitcast.16, bf16[32,512,128]{2,1,0:T(8,128)(2,1)} %weight_hbm.1), custom_call_target="tpu_custom_call" | custom-call | tf_op jit(solution)/shard_map/attend/pallas_call | solution.py:205
  8.7 22.2 %all_to_all.23 = bf16[32,8,256]{2,1,0:T(8,128)(2,1)S(1)} all-to-all(bf16[32,8,256]{2,1,0:T(8,128)(2,1)S(1)} %bitcast.13), channel_id=1, replica_groups=mesh['section'=2,'kv'=32,'head'=4] {'kv'}, dimensions={0} | all-to-all | bytes 262144 | tf_op jit(solution)/shard_map/all_to_all | solution.py:266
  30.9 0.3 combine.1
  31.2 11.8 %all_to_all.24 = bf16[32,8,128]{2,1,0:T(8,128)(2,1)S(1)} all-to-all(bf16[32,8,128]{2,1,0:T(8,128)(2,1)S(1)} %bitcast.15), channel_id=1, replica_groups=mesh['section'=2,'kv'=32,'head'=4] {'kv'}, dimensions={0} | all-to-all | bytes 131072 | tf_op jit(solution)/shard_map/all_to_all | solution.py:268
  43.0 1.6 %collective-permute-start = (bf16[256,128]{1,0:T(8,128)(2,1)S(1)}, bf16[256,128]{1,0:T(8,128)(2,1)S(1)}, u32[]{:S(2)}, u32[]{:S(2)}) collective-permute-start(bf16[256,128]{1,0:T(8,128)(2,1)S(1)} %bitcast.17), channel_id=1, source_target_pairs={{0,128},{128,0},{1,129},{129,1},{2,130},{130,2},{3,131},{131,3},{4... | collective-permute-start | bytes 196616 | tf_op jit(solution)/shard_map/ppermute | solution.py:269
  44.6 0.9 %collective-permute-done = bf16[256,128]{1,0:T(8,128)(2,1)S(1)} collective-permute-done((bf16[256,128]{1,0:T(8,128)(2,1)S(1)}, bf16[256,128]{1,0:T(8,128)(2,1)S(1)}, u32[]{:S(2)}, u32[]{:S(2)}) %collective-permute-start) | collective-permute-done | bytes 65568 | tf_op jit(solution)/shard_map/ppermute | solution.py:269
  45.5 0.0 copy-done
  45.5 0.3 fusion
  45.9 1.3 %collective-permute-start.1 = (f32[16,112]{1,0:T(8,128)S(1)}, f32[16,112]{1,0:T(8,128)S(1)}, u32[]{:S(2)}, u32[]{:S(2)}) collective-permute-start(f32[16,112]{1,0:T(8,128)S(1)} %fusion), channel_id=1, source_target_pairs={{0,1},{1,2},{2,3},{3,0},{4,5},{5,6},{6,7},{7,4},{8,9},{9,10},{10,1... | collective-permute-start | bytes 21512 | tf_op jit(solution)/shard_map/ppermute | solution.py:275
  47.2 1.5 %collective-permute-start.2 = (f32[16,112]{1,0:T(8,128)S(1)}, f32[16,112]{1,0:T(8,128)S(1)}, u32[]{:S(2)}, u32[]{:S(2)}) collective-permute-start(f32[16,112]{1,0:T(8,128)S(1)} %fusion), channel_id=1, source_target_pairs={{0,3},{1,0},{2,1},{3,2},{4,7},{5,4},{6,5},{7,6},{8,11},{9,8},{10,9... | collective-permute-start | bytes 21512 | tf_op jit(solution)/shard_map/ppermute | solution.py:275
  48.7 1.6 %collective-permute-start.3 = (f32[16,112]{1,0:T(8,128)S(1)}, f32[16,112]{1,0:T(8,128)S(1)}, u32[]{:S(2)}, u32[]{:S(2)}) collective-permute-start(f32[16,112]{1,0:T(8,128)S(1)} %fusion), channel_id=1, source_target_pairs={{0,2},{1,3},{2,0},{3,1},{4,6},{5,7},{6,4},{7,5},{8,10},{9,11},{10,... | collective-permute-start | bytes 21512 | tf_op jit(solution)/shard_map/ppermute | solution.py:275
  50.3 0.0 collective-permute-done.1
  50.3 0.0 collective-permute-done.2
  50.3 2.4 %collective-permute-done.3 = f32[16,112]{1,0:T(8,128)S(1)} collective-permute-done((f32[16,112]{1,0:T(8,128)S(1)}, f32[16,112]{1,0:T(8,128)S(1)}, u32[]{:S(2)}, u32[]{:S(2)}) %collective-permute-start.3) | collective-permute-done | bytes 7200 | tf_op jit(solution)/shard_map/ppermute | solution.py:275
  52.7 0.0 copy-done.1
  52.7 0.6 %fusion.4 = bf16[16,112]{1,0:T(8,128)(2,1)} fusion(f32[16,112]{1,0:T(8,128)S(1)} %add_add_fusion, f32[8,112]{1,0:T(8,128)S(1)} %get-tuple-element.6, f32[8,112]{1,0:T(8,128)S(1)} %get-tuple-element.5, bf16[16,112]{1,0:T(8,128)(2,1)S(1)} %copy-done.1, pred[]{:T(512)S(6)} %eq.3), kind=kLoop, calls=%fused_computation.6 | loop fusion | flops 8960 | bytes 21505 | tf_op jit(solution)/shard_map/convert_element_type | solution.py:280
  (2 shorter events, 0.0 us)
Async XLA Ops:
  0.0 45.5 %copy-start = (bf16[4096,112]{0,1:T(8,128)(2,1)S(1)}, bf16[4096,112]{0,1:T(8,128)(2,1)}, u32[]{:S(2)}) copy-start(bf16[4096,112]{0,1:T(8,128)(2,1)} %param.14) | copy-start | bytes 2752516
  0.0 52.7 %copy-start.1 = (bf16[16,112]{1,0:T(8,128)(2,1)S(1)}, bf16[16,112]{1,0:T(8,128)(2,1)}, u32[]{:S(2)}) copy-start(bf16[16,112]{1,0:T(8,128)(2,1)} %param.15) | copy-start | bytes 10756
  43.0 2.5 %collective-permute-start = (bf16[256,128]{1,0:T(8,128)(2,1)S(1)}, bf16[256,128]{1,0:T(8,128)(2,1)S(1)}, u32[]{:S(2)}, u32[]{:S(2)}) collective-permute-start(bf16[256,128]{1,0:T(8,128)(2,1)S(1)} %bitcast.17), channel_id=1, source_target_pairs={{0,128},{128,0},{1,129},{129,1},{2,130},{130,2},{3,131},{131,3},{4... | collective-permute-start | bytes 196616 | tf_op jit(solution)/shard_map/ppermute | solution.py:269
  45.9 4.4 %collective-permute-start.1 = (f32[16,112]{1,0:T(8,128)S(1)}, f32[16,112]{1,0:T(8,128)S(1)}, u32[]{:S(2)}, u32[]{:S(2)}) collective-permute-start(f32[16,112]{1,0:T(8,128)S(1)} %fusion), channel_id=1, source_target_pairs={{0,1},{1,2},{2,3},{3,0},{4,5},{5,6},{6,7},{7,4},{8,9},{9,10},{10,1... | collective-permute-start | bytes 21512 | tf_op jit(solution)/shard_map/ppermute | solution.py:275
  47.2 3.1 %collective-permute-start.2 = (f32[16,112]{1,0:T(8,128)S(1)}, f32[16,112]{1,0:T(8,128)S(1)}, u32[]{:S(2)}, u32[]{:S(2)}) collective-permute-start(f32[16,112]{1,0:T(8,128)S(1)} %fusion), channel_id=1, source_target_pairs={{0,3},{1,0},{2,1},{3,2},{4,7},{5,4},{6,5},{7,6},{8,11},{9,8},{10,9... | collective-permute-start | bytes 21512 | tf_op jit(solution)/shard_map/ppermute | solution.py:275
  48.7 4.0 %collective-permute-start.3 = (f32[16,112]{1,0:T(8,128)S(1)}, f32[16,112]{1,0:T(8,128)S(1)}, u32[]{:S(2)}, u32[]{:S(2)}) collective-permute-start(f32[16,112]{1,0:T(8,128)S(1)} %fusion), channel_id=1, source_target_pairs={{0,2},{1,3},{2,0},{3,1},{4,6},{5,7},{6,4},{7,5},{8,10},{9,11},{10,... | collective-permute-start | bytes 21512 | tf_op jit(solution)/shard_map/ppermute | solution.py:275

commit v7 on v6

--- a/solution.py
+++ b/solution.py
@@ -133,16 +133,17 @@
     for part in range(early):
         blind(part).wait()
 
-    def sweep(step, carry):
+    def sweep(step, carry, between=None):
         wide = lax.div(blocks, jnp.int32(WIDE))
         span = WIDE * UNROLL
         carry = lax.fori_loop(0, wide, lambda k, c: step(span, k * span, c), carry)
+        if between is not None:
+            between()
         return lax.fori_loop(
             wide * WIDE, blocks, lambda k, c: step(UNROLL, k * UNROLL, c), carry
         )
 
-    sweep(score, jnp.int32(0))
-    fetches[4].start()
+    sweep(score, jnp.int32(0), fetches[4].start)
 
     for mine in range(requests):
         top = jnp.max(high[mine], axis=1, keepdims=True)

time: 53.7 us -> 53.8 us (level)
  starting transfers between devices: 6.02 us -> 7.06 us
  Pallas kernels: 8.94 us -> 8.08 us
    ppermute x1, starting transfers between devices: 1.62 us -> 2.66 us  [body(): others = lax.ppermute(values, 'section', [(0, 1), (1, 0)])]
    pallas_call x1, Pallas kernels: 8.65 us -> 7.78 us  [attend(): pl.pallas_call(attend_kernel, out_shape=jax.ShapeDtypeStruct((heads * req...]
    all_to_all x1, blocking collectives: 22.2 us -> 21.7 us  [body(): parts = lax.all_to_all(parts, 'kv', 0, 0, tiled=True)]
where the time goes in v7:
time: 53.8 us; the launch traced here: 53.2 us
  blocking collectives  33.8 us (63%)
  Pallas kernels  8.08 us (15%)
  starting transfers between devices  7.06 us (13%)
  waiting for transfers between devices  3.31 us (6%)
  other arithmetic  0.61 us (1%)
    all_to_all x1, blocking collectives, body(): parts = lax.all_to_all(parts, 'kv', 0, 0, tiled=True)  21.7 us
    all_to_all x1, blocking collectives, body(): values = lax.all_to_all(values, 'kv', 0, 0, tiled=True)  12.1 us
    pallas_call x1, Pallas kernels, attend(): pl.pallas_call(attend_kernel, out_shape=jax.ShapeDtypeStruct((heads * req...  7.78 us
    ppermute x3, starting transfers between devices, body(): lax.ppermute(projected, 'head', [(k, (k + step) % groups) for k in range(...  4.39 us
    ppermute x1, starting transfers between devices, body(): others = lax.ppermute(values, 'section', [(0, 1), (1, 0)])  2.66 us
    ppermute x3, waiting for transfers between devices, body(): lax.ppermute(projected, 'head', [(k, (k + step) % groups) for k in range(...  2.41 us
  transfers between devices with their start and end apart: 4, of which 2 were waited for; matrix products, arithmetic and copies ran while one was open for 0% of the time, Pallas kernels for 0%

profile of v7, /device:TPU:1, one launch (start us, length us, event | category | flops | bytes accessed | tf_op | source)
XLA Modules:
  0.0 53.2 jit_solution(1271556039157350808)
XLA Ops:
  0.0 0.0 copy-start
  0.0 0.0 copy-start.1
  0.0 7.8 %attend.1 = bf16[256,256]{1,0:T(8,128)(2,1)S(1)} custom-call(s32[64]{0:T(128)} %owner_hbm.1, s32[64]{0:T(128)} %page_hbm.1, s32[8]{0:T(128)} %length_hbm.1, bf16[8,32,576]{2,1,0:T(8,128)(2,1)} %query_hbm.1, bf16[64,576,128]{2,1,0:T(8,128)(2,1)} %bitcast.16, bf16[32,512,128]{2,1,0:T(8,128)(2,1)} %weight_hbm.1), custom_call_target="tpu_custom_call" | custom-call | tf_op jit(solution)/shard_map/attend/pallas_call | solution.py:206
  7.8 21.7 %all_to_all.23 = bf16[32,8,256]{2,1,0:T(8,128)(2,1)S(1)} all-to-all(bf16[32,8,256]{2,1,0:T(8,128)(2,1)S(1)} %bitcast.13), channel_id=1, replica_groups=mesh['section'=2,'kv'=32,'head'=4] {'kv'}, dimensions={0} | all-to-all | bytes 262144 | tf_op jit(solution)/shard_map/all_to_all | solution.py:267
  29.5 0.3 combine.1
  29.8 12.1 %all_to_all.24 = bf16[32,8,128]{2,1,0:T(8,128)(2,1)S(1)} all-to-all(bf16[32,8,128]{2,1,0:T(8,128)(2,1)S(1)} %bitcast.15), channel_id=1, replica_groups=mesh['section'=2,'kv'=32,'head'=4] {'kv'}, dimensions={0} | all-to-all | bytes 131072 | tf_op jit(solution)/shard_map/all_to_all | solution.py:269
  41.9 2.7 %collective-permute-start = (bf16[256,128]{1,0:T(8,128)(2,1)S(1)}, bf16[256,128]{1,0:T(8,128)(2,1)S(1)}, u32[]{:S(2)}, u32[]{:S(2)}) collective-permute-start(bf16[256,128]{1,0:T(8,128)(2,1)S(1)} %bitcast.17), channel_id=1, source_target_pairs={{0,128},{128,0},{1,129},{129,1},{2,130},{130,2},{3,131},{131,3},{4... | collective-permute-start | bytes 196616 | tf_op jit(solution)/shard_map/ppermute | solution.py:270
  44.6 0.9 %collective-permute-done = bf16[256,128]{1,0:T(8,128)(2,1)S(1)} collective-permute-done((bf16[256,128]{1,0:T(8,128)(2,1)S(1)}, bf16[256,128]{1,0:T(8,128)(2,1)S(1)}, u32[]{:S(2)}, u32[]{:S(2)}) %collective-permute-start) | collective-permute-done | bytes 65568 | tf_op jit(solution)/shard_map/ppermute | solution.py:270
  45.5 0.0 copy-done
  45.5 0.3 fusion
  45.8 1.3 %collective-permute-start.1 = (f32[16,112]{1,0:T(8,128)S(1)}, f32[16,112]{1,0:T(8,128)S(1)}, u32[]{:S(2)}, u32[]{:S(2)}) collective-permute-start(f32[16,112]{1,0:T(8,128)S(1)} %fusion), channel_id=1, source_target_pairs={{0,1},{1,2},{2,3},{3,0},{4,5},{5,6},{6,7},{7,4},{8,9},{9,10},{10,1... | collective-permute-start | bytes 21512 | tf_op jit(solution)/shard_map/ppermute | solution.py:276
  47.1 1.5 %collective-permute-start.2 = (f32[16,112]{1,0:T(8,128)S(1)}, f32[16,112]{1,0:T(8,128)S(1)}, u32[]{:S(2)}, u32[]{:S(2)}) collective-permute-start(f32[16,112]{1,0:T(8,128)S(1)} %fusion), channel_id=1, source_target_pairs={{0,3},{1,0},{2,1},{3,2},{4,7},{5,4},{6,5},{7,6},{8,11},{9,8},{10,9... | collective-permute-start | bytes 21512 | tf_op jit(solution)/shard_map/ppermute | solution.py:276
  48.6 1.6 %collective-permute-start.3 = (f32[16,112]{1,0:T(8,128)S(1)}, f32[16,112]{1,0:T(8,128)S(1)}, u32[]{:S(2)}, u32[]{:S(2)}) collective-permute-start(f32[16,112]{1,0:T(8,128)S(1)} %fusion), channel_id=1, source_target_pairs={{0,2},{1,3},{2,0},{3,1},{4,6},{5,7},{6,4},{7,5},{8,10},{9,11},{10,... | collective-permute-start | bytes 21512 | tf_op jit(solution)/shard_map/ppermute | solution.py:276
  50.2 0.0 collective-permute-done.1
  50.2 0.0 collective-permute-done.2
  50.2 2.4 %collective-permute-done.3 = f32[16,112]{1,0:T(8,128)S(1)} collective-permute-done((f32[16,112]{1,0:T(8,128)S(1)}, f32[16,112]{1,0:T(8,128)S(1)}, u32[]{:S(2)}, u32[]{:S(2)}) %collective-permute-start.3) | collective-permute-done | bytes 7200 | tf_op jit(solution)/shard_map/ppermute | solution.py:276
  52.6 0.0 copy-done.1
  52.6 0.6 %fusion.4 = bf16[16,112]{1,0:T(8,128)(2,1)} fusion(f32[16,112]{1,0:T(8,128)S(1)} %add_add_fusion, f32[8,112]{1,0:T(8,128)S(1)} %get-tuple-element.6, f32[8,112]{1,0:T(8,128)S(1)} %get-tuple-element.5, bf16[16,112]{1,0:T(8,128)(2,1)S(1)} %copy-done.1, pred[]{:T(512)S(6)} %eq.3), kind=kLoop, calls=%fused_computation.6 | loop fusion | flops 8960 | bytes 21505 | tf_op jit(solution)/shard_map/convert_element_type | solution.py:281
  (2 shorter events, 0.0 us)
Async XLA Ops:
  0.0 45.5 %copy-start = (bf16[4096,112]{0,1:T(8,128)(2,1)S(1)}, bf16[4096,112]{0,1:T(8,128)(2,1)}, u32[]{:S(2)}) copy-start(bf16[4096,112]{0,1:T(8,128)(2,1)} %param.14) | copy-start | bytes 2752516
  0.0 52.6 %copy-start.1 = (bf16[16,112]{1,0:T(8,128)(2,1)S(1)}, bf16[16,112]{1,0:T(8,128)(2,1)}, u32[]{:S(2)}) copy-start(bf16[16,112]{1,0:T(8,128)(2,1)} %param.15) | copy-start | bytes 10756
  41.9 3.6 %collective-permute-start = (bf16[256,128]{1,0:T(8,128)(2,1)S(1)}, bf16[256,128]{1,0:T(8,128)(2,1)S(1)}, u32[]{:S(2)}, u32[]{:S(2)}) collective-permute-start(bf16[256,128]{1,0:T(8,128)(2,1)S(1)} %bitcast.17), channel_id=1, source_target_pairs={{0,128},{128,0},{1,129},{129,1},{2,130},{130,2},{3,131},{131,3},{4... | collective-permute-start | bytes 196616 | tf_op jit(solution)/shard_map/ppermute | solution.py:270
  45.8 4.4 %collective-permute-start.1 = (f32[16,112]{1,0:T(8,128)S(1)}, f32[16,112]{1,0:T(8,128)S(1)}, u32[]{:S(2)}, u32[]{:S(2)}) collective-permute-start(f32[16,112]{1,0:T(8,128)S(1)} %fusion), channel_id=1, source_target_pairs={{0,1},{1,2},{2,3},{3,0},{4,5},{5,6},{6,7},{7,4},{8,9},{9,10},{10,1... | collective-permute-start | bytes 21512 | tf_op jit(solution)/shard_map/ppermute | solution.py:276
  47.1 3.1 %collective-permute-start.2 = (f32[16,112]{1,0:T(8,128)S(1)}, f32[16,112]{1,0:T(8,128)S(1)}, u32[]{:S(2)}, u32[]{:S(2)}) collective-permute-start(f32[16,112]{1,0:T(8,128)S(1)} %fusion), channel_id=1, source_target_pairs={{0,3},{1,0},{2,1},{3,2},{4,7},{5,4},{6,5},{7,6},{8,11},{9,8},{10,9... | collective-permute-start | bytes 21512 | tf_op jit(solution)/shard_map/ppermute | solution.py:276
  48.6 4.0 %collective-permute-start.3 = (f32[16,112]{1,0:T(8,128)S(1)}, f32[16,112]{1,0:T(8,128)S(1)}, u32[]{:S(2)}, u32[]{:S(2)}) collective-permute-start(f32[16,112]{1,0:T(8,128)S(1)} %fusion), channel_id=1, source_target_pairs={{0,2},{1,3},{2,0},{3,1},{4,6},{5,7},{6,4},{7,5},{8,10},{9,11},{10,... | collective-permute-start | bytes 21512 | tf_op jit(solution)/shard_map/ppermute | solution.py:276

commit v8 on v7

--- a/solution.py
+++ b/solution.py
@@ -184,11 +184,11 @@
     def project(block, carry):
         for k in range(GROUP):
             head = block * GROUP + k
-            rows = jnp.concatenate(parts_of(packed[head]), axis=0).astype(jnp.bfloat16)
+            value = packed[head]
+            top = value.astype(jnp.bfloat16).astype(jnp.float32)
+            rows = jnp.concatenate([top, value - top], axis=0).astype(jnp.bfloat16)
             product = jnp.dot(rows, weight_ref[head], preferred_element_type=jnp.float32)
-            values[head, :, :width] = (
-                product[:requests] + product[requests : 2 * requests] + product[2 * requests :]
-            )
+            values[head, :, :width] = product[:requests] + product[requests:]
         return carry
 
     lax.fori_loop(0, heads // GROUP, project, 0)

time: 53.8 us -> 53.2 us (0.989)
    all_to_all x1, blocking collectives: 21.7 us -> 21 us  [body(): parts = lax.all_to_all(parts, 'kv', 0, 0, tiled=True)]
where the time goes in v8:
time: 53.2 us; the launch traced here: 53 us
  blocking collectives  33.7 us (63%)
  Pallas kernels  7.85 us (15%)
  starting transfers between devices  7.15 us (13%)
  waiting for transfers between devices  3.31 us (6%)
  other arithmetic  0.61 us (1%)
    all_to_all x1, blocking collectives, body(): parts = lax.all_to_all(parts, 'kv', 0, 0, tiled=True)  21 us
    all_to_all x1, blocking collectives, body(): values = lax.all_to_all(values, 'kv', 0, 0, tiled=True)  12.6 us
    pallas_call x1, Pallas kernels, attend(): pl.pallas_call(attend_kernel, out_shape=jax.ShapeDtypeStruct((heads * req...  7.56 us
    ppermute x3, starting transfers between devices, body(): lax.ppermute(projected, 'head', [(k, (k + step) % groups) for k in range(...  4.4 us
    ppermute x1, starting transfers between devices, body(): others = lax.ppermute(values, 'section', [(0, 1), (1, 0)])  2.75 us
    ppermute x3, waiting for transfers between devices, body(): lax.ppermute(projected, 'head', [(k, (k + step) % groups) for k in range(...  2.41 us
  transfers between devices with their start and end apart: 4, of which 2 were waited for; matrix products, arithmetic and copies ran while one was open for 0% of the time, Pallas kernels for 0%

profile of v8, /device:TPU:1, one launch (start us, length us, event | category | flops | bytes accessed | tf_op | source)
XLA Modules:
  0.0 53.0 jit_solution(626145005460764106)
XLA Ops:
  0.0 0.0 copy-start
  0.0 0.0 copy-start.1
  0.0 7.6 %attend.1 = bf16[256,256]{1,0:T(8,128)(2,1)S(1)} custom-call(s32[64]{0:T(128)} %owner_hbm.1, s32[64]{0:T(128)} %page_hbm.1, s32[8]{0:T(128)} %length_hbm.1, bf16[8,32,576]{2,1,0:T(8,128)(2,1)} %query_hbm.1, bf16[64,576,128]{2,1,0:T(8,128)(2,1)} %bitcast.16, bf16[32,512,128]{2,1,0:T(8,128)(2,1)} %weight_hbm.1), custom_call_target="tpu_custom_call" | custom-call | tf_op jit(solution)/shard_map/attend/pallas_call | solution.py:206
  7.6 21.0 %all_to_all.23 = bf16[32,8,256]{2,1,0:T(8,128)(2,1)S(1)} all-to-all(bf16[32,8,256]{2,1,0:T(8,128)(2,1)S(1)} %bitcast.13), channel_id=1, replica_groups=mesh['section'=2,'kv'=32,'head'=4] {'kv'}, dimensions={0} | all-to-all | bytes 262144 | tf_op jit(solution)/shard_map/all_to_all | solution.py:267
  28.6 0.3 combine.1
  28.9 12.6 %all_to_all.24 = bf16[32,8,128]{2,1,0:T(8,128)(2,1)S(1)} all-to-all(bf16[32,8,128]{2,1,0:T(8,128)(2,1)S(1)} %bitcast.15), channel_id=1, replica_groups=mesh['section'=2,'kv'=32,'head'=4] {'kv'}, dimensions={0} | all-to-all | bytes 131072 | tf_op jit(solution)/shard_map/all_to_all | solution.py:269
  41.5 2.8 %collective-permute-start = (bf16[256,128]{1,0:T(8,128)(2,1)S(1)}, bf16[256,128]{1,0:T(8,128)(2,1)S(1)}, u32[]{:S(2)}, u32[]{:S(2)}) collective-permute-start(bf16[256,128]{1,0:T(8,128)(2,1)S(1)} %bitcast.17), channel_id=1, source_target_pairs={{0,128},{128,0},{1,129},{129,1},{2,130},{130,2},{3,131},{131,3},{4... | collective-permute-start | bytes 196616 | tf_op jit(solution)/shard_map/ppermute | solution.py:270
  44.3 0.9 %collective-permute-done = bf16[256,128]{1,0:T(8,128)(2,1)S(1)} collective-permute-done((bf16[256,128]{1,0:T(8,128)(2,1)S(1)}, bf16[256,128]{1,0:T(8,128)(2,1)S(1)}, u32[]{:S(2)}, u32[]{:S(2)}) %collective-permute-start) | collective-permute-done | bytes 65568 | tf_op jit(solution)/shard_map/ppermute | solution.py:270
  45.2 0.0 copy-done
  45.2 0.3 fusion
  45.5 1.3 %collective-permute-start.1 = (f32[16,112]{1,0:T(8,128)S(1)}, f32[16,112]{1,0:T(8,128)S(1)}, u32[]{:S(2)}, u32[]{:S(2)}) collective-permute-start(f32[16,112]{1,0:T(8,128)S(1)} %fusion), channel_id=1, source_target_pairs={{0,1},{1,2},{2,3},{3,0},{4,5},{5,6},{6,7},{7,4},{8,9},{9,10},{10,1... | collective-permute-start | bytes 21512 | tf_op jit(solution)/shard_map/ppermute | solution.py:276
  46.9 1.5 %collective-permute-start.2 = (f32[16,112]{1,0:T(8,128)S(1)}, f32[16,112]{1,0:T(8,128)S(1)}, u32[]{:S(2)}, u32[]{:S(2)}) collective-permute-start(f32[16,112]{1,0:T(8,128)S(1)} %fusion), channel_id=1, source_target_pairs={{0,3},{1,0},{2,1},{3,2},{4,7},{5,4},{6,5},{7,6},{8,11},{9,8},{10,9... | collective-permute-start | bytes 21512 | tf_op jit(solution)/shard_map/ppermute | solution.py:276
  48.3 1.6 %collective-permute-start.3 = (f32[16,112]{1,0:T(8,128)S(1)}, f32[16,112]{1,0:T(8,128)S(1)}, u32[]{:S(2)}, u32[]{:S(2)}) collective-permute-start(f32[16,112]{1,0:T(8,128)S(1)} %fusion), channel_id=1, source_target_pairs={{0,2},{1,3},{2,0},{3,1},{4,6},{5,7},{6,4},{7,5},{8,10},{9,11},{10,... | collective-permute-start | bytes 21512 | tf_op jit(solution)/shard_map/ppermute | solution.py:276
  49.9 0.0 collective-permute-done.1
  49.9 0.0 collective-permute-done.2
  49.9 2.4 %collective-permute-done.3 = f32[16,112]{1,0:T(8,128)S(1)} collective-permute-done((f32[16,112]{1,0:T(8,128)S(1)}, f32[16,112]{1,0:T(8,128)S(1)}, u32[]{:S(2)}, u32[]{:S(2)}) %collective-permute-start.3) | collective-permute-done | bytes 7200 | tf_op jit(solution)/shard_map/ppermute | solution.py:276
  52.4 0.0 copy-done.1
  52.4 0.6 %fusion.4 = bf16[16,112]{1,0:T(8,128)(2,1)} fusion(f32[16,112]{1,0:T(8,128)S(1)} %add_add_fusion, f32[8,112]{1,0:T(8,128)S(1)} %get-tuple-element.6, f32[8,112]{1,0:T(8,128)S(1)} %get-tuple-element.5, bf16[16,112]{1,0:T(8,128)(2,1)S(1)} %copy-done.1, pred[]{:T(512)S(6)} %eq.3), kind=kLoop, calls=%fused_computation.6 | loop fusion | flops 8960 | bytes 21505 | tf_op jit(solution)/shard_map/convert_element_type | solution.py:281
  (2 shorter events, 0.0 us)
Async XLA Ops:
  0.0 45.2 %copy-start = (bf16[4096,112]{0,1:T(8,128)(2,1)S(1)}, bf16[4096,112]{0,1:T(8,128)(2,1)}, u32[]{:S(2)}) copy-start(bf16[4096,112]{0,1:T(8,128)(2,1)} %param.14) | copy-start | bytes 2752516
  0.0 52.4 %copy-start.1 = (bf16[16,112]{1,0:T(8,128)(2,1)S(1)}, bf16[16,112]{1,0:T(8,128)(2,1)}, u32[]{:S(2)}) copy-start(bf16[16,112]{1,0:T(8,128)(2,1)} %param.15) | copy-start | bytes 10756
  41.5 3.7 %collective-permute-start = (bf16[256,128]{1,0:T(8,128)(2,1)S(1)}, bf16[256,128]{1,0:T(8,128)(2,1)S(1)}, u32[]{:S(2)}, u32[]{:S(2)}) collective-permute-start(bf16[256,128]{1,0:T(8,128)(2,1)S(1)} %bitcast.17), channel_id=1, source_target_pairs={{0,128},{128,0},{1,129},{129,1},{2,130},{130,2},{3,131},{131,3},{4... | collective-permute-start | bytes 196616 | tf_op jit(solution)/shard_map/ppermute | solution.py:270
  45.5 4.4 %collective-permute-start.1 = (f32[16,112]{1,0:T(8,128)S(1)}, f32[16,112]{1,0:T(8,128)S(1)}, u32[]{:S(2)}, u32[]{:S(2)}) collective-permute-start(f32[16,112]{1,0:T(8,128)S(1)} %fusion), channel_id=1, source_target_pairs={{0,1},{1,2},{2,3},{3,0},{4,5},{5,6},{6,7},{7,4},{8,9},{9,10},{10,1... | collective-permute-start | bytes 21512 | tf_op jit(solution)/shard_map/ppermute | solution.py:276
  46.9 3.1 %collective-permute-start.2 = (f32[16,112]{1,0:T(8,128)S(1)}, f32[16,112]{1,0:T(8,128)S(1)}, u32[]{:S(2)}, u32[]{:S(2)}) collective-permute-start(f32[16,112]{1,0:T(8,128)S(1)} %fusion), channel_id=1, source_target_pairs={{0,3},{1,0},{2,1},{3,2},{4,7},{5,4},{6,5},{7,6},{8,11},{9,8},{10,9... | collective-permute-start | bytes 21512 | tf_op jit(solution)/shard_map/ppermute | solution.py:276
  48.3 4.0 %collective-permute-start.3 = (f32[16,112]{1,0:T(8,128)S(1)}, f32[16,112]{1,0:T(8,128)S(1)}, u32[]{:S(2)}, u32[]{:S(2)}) collective-permute-start(f32[16,112]{1,0:T(8,128)S(1)} %fusion), channel_id=1, source_target_pairs={{0,2},{1,3},{2,0},{3,1},{4,6},{5,7},{6,4},{7,5},{8,10},{9,11},{10,... | collective-permute-start | bytes 21512 | tf_op jit(solution)/shard_map/ppermute | solution.py:276
